TPU v7x, 32 devices: a whole 2x2x4 slice. The times are simulated.
32 devices in a mesh: seq: 8 (over y, x, core), batch: 4 (over z).
Axes of the slice: x: 2, y: 2, z: 4, core: 2. Of those that a mesh axis runs over, the one named last changes fastest.
Arguments:
- tokens: bfloat16 [8, 2048, 1024], P('batch', 'seq'), may hold values from -6 to 6
- cotangent: bfloat16 [8, 2048, 1024], P('batch', 'seq'), may hold values from -6 to 6
- lengths: int32 [8], P('batch'), may hold values from 128 to 2048, as said below
- gate_proj: bfloat16 [1024, 1536], P(('seq', 'batch')), may hold values from -0.1875 to 0.1875
- input_proj: bfloat16 [1024, 1536], P(('seq', 'batch')), may hold values from -0.1875 to 0.1875
- rate_proj: bfloat16 [1536, 1536], P(('seq', 'batch')), may hold values from -0.15625 to 0.15625
- entry_proj: bfloat16 [1536, 1536], P(('seq', 'batch')), may hold values from -0.15625 to 0.15625
- out_proj: bfloat16 [1536, 1024], P(('seq', 'batch')), may hold values from -0.4375 to 0.4375
- ffn_gate: bfloat16 [1024, 3072], P(('seq', 'batch')), may hold values from -0.1875 to 0.1875
- ffn_up: bfloat16 [1024, 3072], P(('seq', 'batch')), may hold values from -0.1875 to 0.1875
- ffn_down: bfloat16 [3072, 1024], P(('seq', 'batch')), may hold values from -0.21875 to 0.21875
- norm_gain: bfloat16 [1024], P(('seq', 'batch')), may hold values from 0.5 to 1.5
- ffn_gain: bfloat16 [1024], P(('seq', 'batch')), may hold values from 0.5 to 1.5
- conv_taps: bfloat16 [4, 1536], P(None, ('seq', 'batch')), may hold values from -3 to 3
- conv_bias: bfloat16 [1536], P(('seq', 'batch')), may hold values from -3 to 3
- rate_bias: bfloat16 [1536], P(('seq', 'batch')), may hold values from -4 to 4
- entry_bias: bfloat16 [1536], P(('seq', 'batch')), may hold values from -4 to 4
- decay_logit: bfloat16 [1536], P(('seq', 'batch')), may hold values from 4 to 13
Outputs:
- block_out: float32 [8, 2048, 1024], P('batch', 'seq')
- token_grad: float32 [8, 2048, 1024], P('batch', 'seq')
- grad_gate_proj: float32 [1024, 1536], P(('seq', 'batch'))
- grad_input_proj: float32 [1024, 1536], P(('seq', 'batch'))
- grad_rate_proj: float32 [1536, 1536], P(('seq', 'batch'))
- grad_entry_proj: float32 [1536, 1536], P(('seq', 'batch'))
- grad_out_proj: float32 [1536, 1024], P(('seq', 'batch'))
- grad_ffn_gate: float32 [1024, 3072], P(('seq', 'batch'))
- grad_ffn_up: float32 [1024, 3072], P(('seq', 'batch'))
- grad_ffn_down: float32 [3072, 1024], P(('seq', 'batch'))
- grad_norm_gain: float32 [1024], P(('seq', 'batch'))
- grad_ffn_gain: float32 [1024], P(('seq', 'batch'))
- grad_conv_taps: float32 [4, 1536], P(None, ('seq', 'batch'))
- grad_conv_bias: float32 [1536], P(('seq', 'batch'))
- grad_rate_bias: float32 [1536], P(('seq', 'batch'))
- grad_entry_bias: float32 [1536], P(('seq', 'batch'))
- grad_decay_logit: float32 [1536], P(('seq', 'batch'))
Inputs may be any that keep to these rules, and one draw needn't show every extreme that they name: `lengths`: among the rows of each batch device (2 consecutive rows) one has length 2048.
All inputs are finite; a program needn't handle non-finite values.
Results may differ from a plain program's by a relative error of at most 0.015.
Values may be sent and summed in bfloat16 or wider, within the bound.
A program may use at most 320 MiB of HBM per device.

v0:
```python
import jax
import jax.numpy as jnp
from jax import lax
from jax.sharding import PartitionSpec as P

MICRO = 2


eps = 1e-06
lru_scale = 8.0


def from_behind(value, axis, steps):
    count = lax.axis_size(axis)
    initial, last = (max(0, -steps), min(count, count - steps))
    return lax.ppermute(value, axis, [(source, source + steps) for source in range(initial, last)])


def entering(array, axis, combine, identity):
    size, place = (lax.axis_size(axis), lax.axis_index(axis))
    everything = jax.tree.map(lambda part: lax.all_gather(part, axis), array)
    start = jax.tree.map(
        lambda part, zero: jnp.broadcast_to(jnp.asarray(zero, part.dtype), part.shape),
        array,
        identity,
    )

    def entering_turn(k, before):
        reached = k < place
        new = combine(before, jax.tree.map(lambda part: part[k], everything))
        return jax.tree.map(lambda a, b: jnp.where(reached, a, b), new, before)

    return lax.fori_loop(0, size, entering_turn, start)


def carried_in(array, axis, combine, identity):
    size, place = (lax.axis_size(axis), lax.axis_index(axis))
    everything = jax.tree.map(
        lambda part, kind: lax.all_gather(part.astype(kind), axis),
        array,
        (jnp.bfloat16, jnp.bfloat16),
    )
    start = jax.tree.map(
        lambda part, zero: jnp.broadcast_to(jnp.asarray(zero, part.dtype), part.shape),
        array,
        identity,
    )

    def carried_turn(k, before):
        at = size - 1 - k
        reached = at > place
        new = combine(
            before, jax.tree.map(lambda part, own: part[at].astype(own.dtype), everything, array)
        )
        return jax.tree.map(lambda a, b: jnp.where(reached, a, b), new, before)

    return lax.fori_loop(0, size, carried_turn, start)


def for_sending(array):

    def short(part):
        return part.astype(jnp.bfloat16) if part.dtype == jnp.float32 else part

    return jax.tree.map(short, array)


def project(left, right):
    return jnp.einsum("btd,de->bte", left, right, preferred_element_type=jnp.float32)


def project_back(left, right):
    return jnp.einsum("bte,de->btd", left, right, preferred_element_type=jnp.float32)


def outer_sum(left, right):
    return jnp.einsum("btd,bte->de", left, right, preferred_element_type=jnp.float32)


def link(earlier, later):
    return (earlier[0] * later[0], later[0] * earlier[1] + later[1])


def norm_back(value, scale, gain, grad):
    weighted = grad * gain
    gain_grad = jnp.sum(grad * value * scale, axis=(0, 1))
    spread = jnp.mean(weighted * value, axis=-1, keepdims=True)
    return (scale * weighted - value * scale**3 * spread, gain_grad)


def fetch(shards):
    (
        gate_proj,
        input_proj,
        rate_proj,
        entry_proj,
        out_proj,
        ffn_gate,
        ffn_up,
        ffn_down,
        norm_gain,
        ffn_gain,
        conv_taps,
        conv_bias,
        rate_bias,
        entry_bias,
        decay_logit,
    ) = shards
    return (
        lax.all_gather(gate_proj, ("seq", "batch"), axis=0, tiled=True),
        lax.all_gather(input_proj, ("seq", "batch"), axis=0, tiled=True),
        lax.all_gather(rate_proj, ("seq", "batch"), axis=0, tiled=True),
        lax.all_gather(entry_proj, ("seq", "batch"), axis=0, tiled=True),
        lax.all_gather(out_proj, ("seq", "batch"), axis=0, tiled=True),
        lax.all_gather(ffn_gate, ("seq", "batch"), axis=0, tiled=True),
        lax.all_gather(ffn_up, ("seq", "batch"), axis=0, tiled=True),
        lax.all_gather(ffn_down, ("seq", "batch"), axis=0, tiled=True),
        lax.all_gather(norm_gain, ("seq", "batch"), axis=0, tiled=True),
        lax.all_gather(ffn_gain, ("seq", "batch"), axis=0, tiled=True),
        lax.all_gather(conv_taps, ("seq", "batch"), axis=1, tiled=True),
        lax.all_gather(conv_bias, ("seq", "batch"), axis=0, tiled=True),
        lax.all_gather(rate_bias, ("seq", "batch"), axis=0, tiled=True),
        lax.all_gather(entry_bias, ("seq", "batch"), axis=0, tiled=True),
        lax.all_gather(decay_logit, ("seq", "batch"), axis=0, tiled=True),
    )


def forward_part(tokens, mask, weights):
    (
        gate_proj,
        input_proj,
        rate_proj,
        entry_proj,
        out_proj,
        ffn_gate,
        ffn_up,
        ffn_down,
        norm_gain,
        ffn_gain,
        conv_taps,
        conv_bias,
        rate_bias,
        entry_bias,
        decay_logit,
    ) = weights
    width = tokens.shape[1]
    taps_count = conv_taps.shape[0]
    values = tokens.astype(jnp.float32)
    scale_one = lax.rsqrt(jnp.mean(values * values, axis=-1, keepdims=True) + eps)
    normed = (values * scale_one * norm_gain).astype(jnp.bfloat16)
    gate_pre = project(normed, gate_proj)
    inner = project(normed, input_proj)
    rim = from_behind(inner[:, width - (taps_count - 1) :], "seq", 1)
    extended = jnp.concatenate([rim, inner], axis=1)
    conv = jnp.zeros_like(inner) + conv_bias
    for lag in range(taps_count):
        start = taps_count - 1 - lag
        conv = conv + conv_taps[lag] * extended[:, start : start + width]
    mixed = conv.astype(jnp.bfloat16)
    mixed_full = mixed.astype(jnp.float32)
    rate = jax.nn.sigmoid(project(mixed, rate_proj) + rate_bias)
    entry = jax.nn.sigmoid(project(mixed, entry_proj) + entry_bias)
    logit = decay_logit.astype(jnp.float32)
    log_decay = -lru_scale * jax.nn.softplus(-logit) * rate
    decay = jnp.exp(mask * log_decay)
    root = jnp.sqrt(-jnp.expm1(2.0 * log_decay))
    drive = mask * root * entry * mixed_full
    reach, local = lax.associative_scan(link, (decay, drive), axis=1)
    unit_state = (jnp.ones_like(reach[:, -1]), jnp.zeros_like(local[:, -1]))
    start_state = entering((reach[:, -1], local[:, -1]), "seq", link, unit_state)[1]
    states = local + reach * start_state[:, None]
    gated = (states * jax.nn.gelu(gate_pre)).astype(jnp.bfloat16)
    first = values + project(gated, out_proj)
    scale_two = lax.rsqrt(jnp.mean(first * first, axis=-1, keepdims=True) + eps)
    normed_two = (first * scale_two * ffn_gain).astype(jnp.bfloat16)
    up_pre = project(normed_two, ffn_gate)
    mix_pre = project(normed_two, ffn_up)
    hidden = (jax.nn.gelu(up_pre) * mix_pre).astype(jnp.bfloat16)
    block_out = mask * (first + project(hidden, ffn_down))
    saved = (
        values,
        scale_one,
        normed,
        gate_pre,
        extended,
        mixed,
        mixed_full,
        rate,
        entry,
        log_decay,
        decay,
        root,
        start_state,
        states,
        gated,
        first,
        scale_two,
        normed_two,
        up_pre,
        mix_pre,
        hidden,
    )
    return (block_out, saved)


def backward_part(cotangent, mask, weights, saved):
    (
        gate_proj,
        input_proj,
        rate_proj,
        entry_proj,
        out_proj,
        ffn_gate,
        ffn_up,
        ffn_down,
        norm_gain,
        ffn_gain,
        conv_taps,
        conv_bias,
        rate_bias,
        entry_bias,
        decay_logit,
    ) = weights
    (
        values,
        scale_one,
        normed,
        gate_pre,
        extended,
        mixed,
        mixed_full,
        rate,
        entry,
        log_decay,
        decay,
        root,
        start_state,
        states,
        gated,
        first,
        scale_two,
        normed_two,
        up_pre,
        mix_pre,
        hidden,
    ) = saved
    width = values.shape[1]
    taps_count = conv_taps.shape[0]
    cot_full = mask * cotangent.astype(jnp.float32)
    cot_low = cot_full.astype(jnp.bfloat16)
    grad_ffn_down = outer_sum(hidden, cot_low)
    d_hidden = project_back(cot_low, ffn_down)
    gelu_up, gelu_pull = jax.vjp(jax.nn.gelu, up_pre)
    d_up = gelu_pull(d_hidden * mix_pre)[0].astype(jnp.bfloat16)
    d_mix = (d_hidden * gelu_up).astype(jnp.bfloat16)
    grad_ffn_gate = outer_sum(normed_two, d_up)
    grad_ffn_up = outer_sum(normed_two, d_mix)
    d_normed_two = project_back(d_up, ffn_gate) + project_back(d_mix, ffn_up)
    back_two, grad_ffn_gain = norm_back(first, scale_two, ffn_gain, d_normed_two)
    d_first = cot_full + back_two
    d_first_low = d_first.astype(jnp.bfloat16)
    grad_out_proj = outer_sum(gated, d_first_low)
    d_gated = project_back(d_first_low, out_proj)
    gate, gate_pull = jax.vjp(jax.nn.gelu, gate_pre)
    d_states = d_gated * gate
    d_gate_pre = gate_pull(d_gated * states)[0].astype(jnp.bfloat16)
    following = jnp.concatenate([decay[:, 1:], jnp.ones_like(decay[:, :1])], axis=1)
    reach_back, local_back = lax.associative_scan(link, (following, d_states), reverse=True, axis=1)
    unit_grad = (jnp.ones_like(decay[:, 0]), jnp.zeros_like(decay[:, 0]))
    end_grad = carried_in(
        (decay[:, 0] * reach_back[:, 0], decay[:, 0] * local_back[:, 0]), "seq", link, unit_grad
    )[1]
    carried = local_back + reach_back * end_grad[:, None]
    previous = jnp.concatenate([start_state[:, None], states[:, :-1]], axis=1)
    masked_grad = mask * carried
    d_log = (
        masked_grad * previous * decay
        - masked_grad * entry * mixed_full * jnp.exp(2.0 * log_decay) / root
    )
    logit = decay_logit.astype(jnp.float32)
    grad_decay_logit = jnp.sum(lru_scale * d_log * rate * jax.nn.sigmoid(-logit), axis=(0, 1))
    d_rate_pre = -lru_scale * jax.nn.softplus(-logit) * d_log * rate * (1.0 - rate)
    d_entry_pre = masked_grad * root * mixed_full * entry * (1.0 - entry)
    grad_rate_bias = jnp.sum(d_rate_pre, axis=(0, 1))
    grad_entry_bias = jnp.sum(d_entry_pre, axis=(0, 1))
    rate_low = d_rate_pre.astype(jnp.bfloat16)
    entry_low = d_entry_pre.astype(jnp.bfloat16)
    grad_rate_proj = outer_sum(mixed, rate_low)
    grad_entry_proj = outer_sum(mixed, entry_low)
    d_mixed = (
        masked_grad * root * entry
        + project_back(rate_low, rate_proj)
        + project_back(entry_low, entry_proj)
    )
    grad_conv_bias = jnp.sum(d_mixed, axis=(0, 1))
    tap_grads = []
    for lag in range(taps_count):
        start = taps_count - 1 - lag
        tap_grads.append(jnp.sum(d_mixed * extended[:, start : start + width], axis=(0, 1)))
    grad_conv_taps = jnp.stack(tap_grads, axis=0)
    rim_back = from_behind(for_sending(d_mixed[:, : taps_count - 1]), "seq", -1)
    later = jnp.concatenate([d_mixed, rim_back], axis=1)
    d_inner = jnp.zeros_like(d_mixed)
    for lag in range(taps_count):
        d_inner = d_inner + conv_taps[lag] * later[:, lag : lag + width]
    d_inner = d_inner.astype(jnp.bfloat16)
    grad_input_proj = outer_sum(normed, d_inner)
    grad_gate_proj = outer_sum(normed, d_gate_pre)
    d_normed = project_back(d_gate_pre, gate_proj) + project_back(d_inner, input_proj)
    back_one, grad_norm_gain = norm_back(values, scale_one, norm_gain, d_normed)
    token_grad = d_first + back_one
    grads = (
        grad_gate_proj,
        grad_input_proj,
        grad_rate_proj,
        grad_entry_proj,
        grad_out_proj,
        grad_ffn_gate,
        grad_ffn_up,
        grad_ffn_down,
        grad_norm_gain,
        grad_ffn_gain,
        grad_conv_taps,
        grad_conv_bias,
        grad_rate_bias,
        grad_entry_bias,
        grad_decay_logit,
    )
    return (token_grad, grads)


def reduce_grads(totals):
    shaped = []
    for index, item in enumerate(totals):
        if index == 10:
            item = item.T
        if item.ndim == 1:
            item = item[:, None]
        shaped.append(item[None])
    spread = (
        lax.all_to_all(
            shaped[0].astype(jnp.bfloat16), "seq", split_axis=1, concat_axis=0, tiled=True
        ).astype(jnp.float32),
        lax.all_to_all(
            shaped[1].astype(jnp.bfloat16), "seq", split_axis=1, concat_axis=0, tiled=True
        ).astype(jnp.float32),
        lax.all_to_all(
            shaped[2].astype(jnp.bfloat16), "seq", split_axis=1, concat_axis=0, tiled=True
        ).astype(jnp.float32),
        lax.all_to_all(
            shaped[3].astype(jnp.bfloat16), "seq", split_axis=1, concat_axis=0, tiled=True
        ).astype(jnp.float32),
        lax.all_to_all(
            shaped[4].astype(jnp.bfloat16), "seq", split_axis=1, concat_axis=0, tiled=True
        ).astype(jnp.float32),
        lax.all_to_all(
            shaped[5].astype(jnp.bfloat16), "seq", split_axis=1, concat_axis=0, tiled=True
        ).astype(jnp.float32),
        lax.all_to_all(
            shaped[6].astype(jnp.bfloat16), "seq", split_axis=1, concat_axis=0, tiled=True
        ).astype(jnp.float32),
        lax.all_to_all(
            shaped[7].astype(jnp.bfloat16), "seq", split_axis=1, concat_axis=0, tiled=True
        ).astype(jnp.float32),
        lax.all_to_all(
            shaped[8].astype(jnp.bfloat16), "seq", split_axis=1, concat_axis=0, tiled=True
        ).astype(jnp.float32),
        lax.all_to_all(
            shaped[9].astype(jnp.bfloat16), "seq", split_axis=1, concat_axis=0, tiled=True
        ).astype(jnp.float32),
        lax.all_to_all(for_sending(shaped[10]), "seq", split_axis=1, concat_axis=0, tiled=True),
        lax.all_to_all(for_sending(shaped[11]), "seq", split_axis=1, concat_axis=0, tiled=True),
        lax.all_to_all(for_sending(shaped[12]), "seq", split_axis=1, concat_axis=0, tiled=True),
        lax.all_to_all(for_sending(shaped[13]), "seq", split_axis=1, concat_axis=0, tiled=True),
        lax.all_to_all(for_sending(shaped[14]), "seq", split_axis=1, concat_axis=0, tiled=True),
    )
    folded = [jnp.sum(piece, axis=0) for piece in spread]
    summed = (
        lax.psum_scatter(
            folded[0].astype(jnp.bfloat16), "batch", scatter_dimension=0, tiled=True
        ).astype(jnp.float32),
        lax.psum_scatter(
            folded[1].astype(jnp.bfloat16), "batch", scatter_dimension=0, tiled=True
        ).astype(jnp.float32),
        lax.psum_scatter(
            folded[2].astype(jnp.bfloat16), "batch", scatter_dimension=0, tiled=True
        ).astype(jnp.float32),
        lax.psum_scatter(
            folded[3].astype(jnp.bfloat16), "batch", scatter_dimension=0, tiled=True
        ).astype(jnp.float32),
        lax.psum_scatter(
            folded[4].astype(jnp.bfloat16), "batch", scatter_dimension=0, tiled=True
        ).astype(jnp.float32),
        lax.psum_scatter(
            folded[5].astype(jnp.bfloat16), "batch", scatter_dimension=0, tiled=True
        ).astype(jnp.float32),
        lax.psum_scatter(
            folded[6].astype(jnp.bfloat16), "batch", scatter_dimension=0, tiled=True
        ).astype(jnp.float32),
        lax.psum_scatter(
            folded[7].astype(jnp.bfloat16), "batch", scatter_dimension=0, tiled=True
        ).astype(jnp.float32),
        lax.psum_scatter(
            folded[8].astype(jnp.bfloat16), "batch", scatter_dimension=0, tiled=True
        ).astype(jnp.float32),
        lax.psum_scatter(
            folded[9].astype(jnp.bfloat16), "batch", scatter_dimension=0, tiled=True
        ).astype(jnp.float32),
        lax.psum_scatter(
            folded[10].astype(jnp.bfloat16), "batch", scatter_dimension=0, tiled=True
        ).astype(jnp.float32),
        lax.psum_scatter(
            folded[11].astype(jnp.bfloat16), "batch", scatter_dimension=0, tiled=True
        ).astype(jnp.float32),
        lax.psum_scatter(
            folded[12].astype(jnp.bfloat16), "batch", scatter_dimension=0, tiled=True
        ).astype(jnp.float32),
        lax.psum_scatter(
            folded[13].astype(jnp.bfloat16), "batch", scatter_dimension=0, tiled=True
        ).astype(jnp.float32),
        lax.psum_scatter(
            folded[14].astype(jnp.bfloat16), "batch", scatter_dimension=0, tiled=True
        ).astype(jnp.float32),
    )
    result = []
    for index, item in enumerate(summed):
        if index == 10:
            result.append(item.T)
        elif totals[index].ndim == 1:
            result.append(item[:, 0])
        else:
            result.append(item)
    return tuple(result)


def per_device(
    tokens,
    cotangent,
    lengths,
    gate_proj,
    input_proj,
    rate_proj,
    entry_proj,
    out_proj,
    ffn_gate,
    ffn_up,
    ffn_down,
    norm_gain,
    ffn_gain,
    conv_taps,
    conv_bias,
    rate_bias,
    entry_bias,
    decay_logit,
):
    shards = (
        gate_proj,
        input_proj,
        rate_proj,
        entry_proj,
        out_proj,
        ffn_gate,
        ffn_up,
        ffn_down,
        norm_gain,
        ffn_gain,
        conv_taps,
        conv_bias,
        rate_bias,
        entry_bias,
        decay_logit,
    )
    rows, width = (tokens.shape[0], tokens.shape[1])
    place = lax.axis_index("seq") * width + lax.iota(jnp.int32, width)
    mask_all = (place[None, :] < lengths[:, None]).astype(jnp.float32)[:, :, None]
    group = rows // MICRO
    totals = None
    block_parts = []
    grad_parts = []
    for part in range(MICRO):
        lower = part * group
        mask = mask_all[lower : lower + group]
        weights = fetch(shards)
        block_out, saved = forward_part(tokens[lower : lower + group], mask, weights)
        weights = fetch(shards)
        token_grad, grads = backward_part(cotangent[lower : lower + group], mask, weights, saved)
        totals = grads if part == 0 else jax.tree.map(jnp.add, totals, grads)
        block_parts.append(block_out)
        grad_parts.append(token_grad)
    summed = reduce_grads(totals)
    return (jnp.concatenate(block_parts, axis=0), jnp.concatenate(grad_parts, axis=0)) + summed


def solution(mesh):
    placed = (
        P("batch", "seq", None),
        P("batch", "seq", None),
        P("batch"),
        P(("seq", "batch"), None),
        P(("seq", "batch"), None),
        P(("seq", "batch"), None),
        P(("seq", "batch"), None),
        P(("seq", "batch"), None),
        P(("seq", "batch"), None),
        P(("seq", "batch"), None),
        P(("seq", "batch"), None),
        P(("seq", "batch")),
        P(("seq", "batch")),
        P(None, ("seq", "batch")),
        P(("seq", "batch")),
        P(("seq", "batch")),
        P(("seq", "batch")),
        P(("seq", "batch")),
    )
    return jax.shard_map(
        per_device,
        mesh=mesh,
        in_specs=placed,
        out_specs=(
            P("batch", "seq", None),
            P("batch", "seq", None),
            P(("seq", "batch"), None),
            P(("seq", "batch"), None),
            P(("seq", "batch"), None),
            P(("seq", "batch"), None),
            P(("seq", "batch"), None),
            P(("seq", "batch"), None),
            P(("seq", "batch"), None),
            P(("seq", "batch"), None),
            P(("seq", "batch")),
            P(("seq", "batch")),
            P(None, ("seq", "batch")),
            P(("seq", "batch")),
            P(("seq", "batch")),
            P(("seq", "batch")),
            P(("seq", "batch")),
        ),
        check_vma=False,
    )
```

profile of v0, /device:TPU:16, one launch (start us, length us, event | category | flops | bytes accessed | tf_op | source)
XLA Modules:
  0.0 2405.9 jit_solution(13677791823139495227)
XLA Ops:
  17.8 40.9 %all-reduce.138 = (bf16[1024]{0:T(1024)(128)(2,1)S(1)}, bf16[1536]{0:T(1024)(128)(2,1)S(1)}, bf16[1536]{0:T(1024)(128)(2,1)S(1)}, bf16[1536]{0:T(1024)(128)(2,1)...) all-reduce(bf16[1024]{0:T(1024)(128)(2,1)S(1)} %dynamic-update-slic, ...), channel_id=1, replica_groups=mesh['seq'=8,'batch'=4] {'seq','batch'}, use_global_device_ids=true, to_apply=%add.134 | all-reduce | flops 8192 | bytes 32768
  60.2 62.4 %all-gather = bf16[32,48,4]{1,2,0:T(4,128)(2,1)S(1)} all-gather(bf16[1,48,4]{1,2,0:T(4,128)(2,1)S(1)} %bitcast.672), channel_id=1, replica_groups=mesh['seq'=8,'batch'=4] {'seq','batch'}, dimensions={0}, use_global_device_ids=true | all-gather | bytes 12672 | tf_op jit(solution)/shard_map/all_gather | solution.py:120
  140.3 56.7 %all-gather.12.cloned.1.call-done = bf16[1536,1536]{1,0:T(8,128)(2,1)} async-done(((bf16[48,1536]{1,0:T(8,128)(2,1)}), bf16[1536,1536]{1,0:T(8,128)(2,1)}) %all-gather.12.cloned.1.call-update) | async-done | bytes 4718608 | tf_op jit(solution)/shard_map/all_gather | solution.py:112
  203.9 58.2 %all-gather.14.cloned.1.call-done = bf16[1536,1536]{1,0:T(8,128)(2,1)} async-done(((bf16[48,1536]{1,0:T(8,128)(2,1)}), bf16[1536,1536]{1,0:T(8,128)(2,1)}) %all-gather.14.cloned.1.call-update) | async-done | bytes 4718608 | tf_op jit(solution)/shard_map/all_gather | solution.py:113
  411.9 11.1 slice.1210
  741.0 10.0 multiply_convert_fusion.1
  1178.4 12.9 rev.18
  1217.1 13.0 rev.16
  1372.8 10.5 reduce.85
  1394.0 21.7 copy.104
  1415.7 20.0 reduce.81
  1450.9 35.0 %copy.106 = bf16[1,1024,1536]{2,0,1:T(2,128)(2,1)} copy(bf16[1,1024,1536]{2,1,0:T(8,128)(2,1)S(1)} %fusion.7) | data formatting | bytes 6291456 | tf_op jit(solution)/shard_map/convert_element_type | solution.py:342
  1485.9 22.0 reduce.77
  1523.3 35.0 %copy.105 = bf16[1,1024,1536]{2,0,1:T(2,128)(2,1)} copy(bf16[1,1024,1536]{2,1,0:T(8,128)(2,1)S(1)} %fusion.8) | data formatting | bytes 6291456 | tf_op jit(solution)/shard_map/convert_element_type | solution.py:345
  1558.3 22.0 reduce.78
  1596.1 52.2 %copy.102 = bf16[1,1536,1536]{2,0,1:T(2,128)(2,1)} copy(bf16[1,1536,1536]{2,1,0:T(8,128)(2,1)S(1)} %fusion.2) | data formatting | bytes 9437184 | tf_op jit(solution)/shard_map/convert_element_type | solution.py:351
  1648.3 31.9 %reduce.80 = bf16[1536,1536]{1,0:T(8,128)(2,1)} reduce(bf16[1536,1,1536]{2,1,0:T(2,128)(2,1)} %bitcast.626, bf16[]{:T(256)} %broadcast.782), dimensions={1}, to_apply=%bitcast.591.reduce_sub_computation | reduce | bytes 9437186
  1697.8 52.2 %copy.103 = bf16[1,1536,1536]{2,0,1:T(2,128)(2,1)} copy(bf16[1,1536,1536]{2,1,0:T(8,128)(2,1)S(1)} %fusion.3) | data formatting | bytes 9437184 | tf_op jit(solution)/shard_map/convert_element_type | solution.py:348
  1750.0 31.9 %reduce.79 = bf16[1536,1536]{1,0:T(8,128)(2,1)} reduce(bf16[1536,1,1536]{2,1,0:T(2,128)(2,1)} %bitcast.627, bf16[]{:T(256)} %broadcast.782), dimensions={1}, to_apply=%bitcast.592.reduce_sub_computation | reduce | bytes 9437186
  1800.6 57.7 %copy.101 = bf16[1,1024,3072]{2,0,1:T(2,128)(2,1)} copy(bf16[1,1024,3072]{2,1,0:T(8,128)(2,1)S(1)} %fusion.4) | data formatting | bytes 12582912 | tf_op jit(solution)/shard_map/convert_element_type | solution.py:357
  1858.3 37.9 %reduce.82 = bf16[1024,3072]{1,0:T(8,128)(2,1)} reduce(bf16[1024,1,3072]{2,1,0:T(2,128)(2,1)} %bitcast.618, bf16[]{:T(256)} %broadcast.782), dimensions={1}, to_apply=%bitcast.590.reduce_sub_computation | reduce | bytes 12582914
  1915.9 57.7 %copy.100 = bf16[1,1024,3072]{2,0,1:T(2,128)(2,1)} copy(bf16[1,1024,3072]{2,1,0:T(8,128)(2,1)S(1)} %fusion.5) | data formatting | bytes 12582912 | tf_op jit(solution)/shard_map/convert_element_type | solution.py:360
  1973.6 37.8 %reduce.83 = bf16[1024,3072]{1,0:T(8,128)(2,1)} reduce(bf16[1024,1,3072]{2,1,0:T(2,128)(2,1)} %bitcast.619, bf16[]{:T(256)} %broadcast.782), dimensions={1}, to_apply=%bitcast.589.reduce_sub_computation | reduce | bytes 12582914
  2029.6 12.7 reduce.72
  2043.2 12.5 reduce.70
  2056.6 12.9 reduce.71
  2074.4 12.5 reduce.69
  2164.8 42.6 %copy.99 = bf16[1,3072,1024]{2,0,1:T(2,128)(2,1)} copy(bf16[1,3072,1024]{2,1,0:T(8,128)(2,1)S(1)} %fusion.6) | data formatting | bytes 12582912 | tf_op jit(solution)/shard_map/convert_element_type | solution.py:363
  2207.4 37.8 %reduce.84 = bf16[3072,1024]{1,0:T(8,128)(2,1)} reduce(bf16[3072,1,1024]{2,1,0:T(2,128)(2,1)} %bitcast.617, bf16[]{:T(256)} %broadcast.782), dimensions={1}, to_apply=%bitcast.588.reduce_sub_computation | reduce | bytes 12582914
  2280.2 11.0 reshape.887
  2306.0 11.5 reshape.889
  2348.6 11.2 reshape.891
  (1363 shorter events, 1433.5 us)
Async XLA Ops:
  7.2 116.9 %all-gather.10.cloned.1.call-start = ((), (), s32[]{:S(2)}) async-start(), calls=%async_computation.30 | async-start | bytes 3244032 | tf_op jit(solution)/shard_map/all_gather | solution.py:111
  8.0 123.1 %all-gather.16.cloned.1.call-start = ((), (), s32[]{:S(2)}) async-start(), calls=%async_computation.33 | async-start | bytes 3244032 | tf_op jit(solution)/shard_map/all_gather | solution.py:110
  8.7 188.3 %all-gather.12.cloned.1.call-start = ((), (), s32[]{:S(2)}) async-start(), calls=%async_computation.31 | async-start | bytes 4866048 | tf_op jit(solution)/shard_map/all_gather | solution.py:112
  9.4 252.6 %all-gather.14.cloned.1.call-start = ((), (), s32[]{:S(2)}) async-start(), calls=%async_computation.32 | async-start | bytes 4866048 | tf_op jit(solution)/shard_map/all_gather | solution.py:113
  10.0 708.2 %all-gather.18.cloned.1.call-start = ((), (), s32[]{:S(2)}) async-start(), calls=%async_computation.34 | async-start | bytes 3244032 | tf_op jit(solution)/shard_map/all_gather | solution.py:114
  10.6 717.6 %all-gather.20.cloned.1.call-start = ((), (), s32[]{:S(2)}) async-start(), calls=%async_computation.35 | async-start | bytes 6488064 | tf_op jit(solution)/shard_map/all_gather | solution.py:115
  11.2 723.5 %all-gather.22.cloned.1.call-start = ((), (), s32[]{:S(2)}) async-start(), calls=%async_computation.36 | async-start | bytes 6488064 | tf_op jit(solution)/shard_map/all_gather | solution.py:116
  11.9 729.1 %all-gather.24.cloned.1.call-start = ((), (), s32[]{:S(2)}) async-start(), calls=%async_computation.37 | async-start | bytes 6488064 | tf_op jit(solution)/shard_map/all_gather | solution.py:117
  1385.4 57.3 %all-to-all-start.10 = ((bf16[8,2,384]{2,1,0:T(2,128)(2,1)}), bf16[8,2,384]{2,1,0:T(2,128)(2,1)S(1)}, u32[]{:S(2)}, u32[]{:S(2)}) async-start(bf16[8,2,384]{2,1,0:T(2,128)(2,1)} %reshape.892), calls=%async_computation.18 | async-start | bytes 24576 | tf_op jit(solution)/shard_map/all_to_all | solution.py:371
  1442.8 72.2 %all-to-all-start.4 = ((bf16[8,2,98304]{2,1,0:T(2,128)(2,1)}), bf16[8,2,98304]{2,1,0:T(2,128)(2,1)}, u32[]{:S(2)}, u32[]{:S(2)}) async-start(bf16[8,2,98304]{2,1,0:T(2,128)(2,1)} %reshape.884), calls=%async_computation.8 | async-start | bytes 6291456 | tf_op jit(solution)/shard_map/all_to_all | solution.py:353
  1515.0 72.3 %all-to-all-start = ((bf16[8,2,98304]{2,1,0:T(2,128)(2,1)}), bf16[8,2,98304]{2,1,0:T(2,128)(2,1)}, u32[]{:S(2)}, u32[]{:S(2)}) async-start(bf16[8,2,98304]{2,1,0:T(2,128)(2,1)} %reshape.876), calls=%async_computation | async-start | bytes 6291456 | tf_op jit(solution)/shard_map/all_to_all | solution.py:341
  1587.3 101.1 %all-to-all-start.1 = ((bf16[8,2,98304]{2,1,0:T(2,128)(2,1)}), bf16[8,2,98304]{2,1,0:T(2,128)(2,1)}, u32[]{:S(2)}, u32[]{:S(2)}) async-start(bf16[8,2,98304]{2,1,0:T(2,128)(2,1)} %reshape.878), calls=%async_computation.2 | async-start | bytes 6291456 | tf_op jit(solution)/shard_map/all_to_all | solution.py:344
  1688.4 101.7 %all-to-all-start.3 = ((bf16[8,2,147456]{2,1,0:T(2,128)(2,1)}), bf16[8,2,147456]{2,1,0:T(2,128)(2,1)}, u32[]{:S(2)}, u32[]{:S(2)}) async-start(bf16[8,2,147456]{2,1,0:T(2,128)(2,1)} %reshape.882), calls=%async_computation.6 | async-start | bytes 9437184 | tf_op jit(solution)/shard_map/all_to_all | solution.py:350
  1790.1 115.5 %all-to-all-start.2 = ((bf16[8,2,147456]{2,1,0:T(2,128)(2,1)}), bf16[8,2,147456]{2,1,0:T(2,128)(2,1)}, u32[]{:S(2)}, u32[]{:S(2)}) async-start(bf16[8,2,147456]{2,1,0:T(2,128)(2,1)} %reshape.880), calls=%async_computation.4 | async-start | bytes 9437184 | tf_op jit(solution)/shard_map/all_to_all | solution.py:347
  1905.6 115.1 %all-to-all-start.5 = ((bf16[8,2,196608]{2,1,0:T(2,128)(2,1)}), bf16[8,2,196608]{2,1,0:T(2,128)(2,1)}, u32[]{:S(2)}, u32[]{:S(2)}) async-start(bf16[8,2,196608]{2,1,0:T(2,128)(2,1)} %reshape.886), calls=%async_computation.10 | async-start | bytes 12582912 | tf_op jit(solution)/shard_map/all_to_all | solution.py:356
  2020.7 233.8 %all-to-all-start.6 = ((bf16[8,2,196608]{2,1,0:T(2,128)(2,1)}), bf16[8,2,196608]{2,1,0:T(2,128)(2,1)}, u32[]{:S(2)}, u32[]{:S(2)}) async-start(bf16[8,2,196608]{2,1,0:T(2,128)(2,1)} %reshape.888), calls=%async_computation.12 | async-start | bytes 12582912 | tf_op jit(solution)/shard_map/all_to_all | solution.py:359
  2025.5 318.4 %reduce-scatter.48.cloned.1.call-start = ((), (), s32[]{:S(2)}) async-start(), calls=%async_computation.47 | async-start | bytes 40960
  2029.5 315.7 %reduce-scatter.58.cloned.1.call-start = ((), (), s32[]{:S(2)}) async-start(), calls=%async_computation.52 | async-start | bytes 61440
  2043.1 302.9 %reduce-scatter.54.cloned.1.call-start = ((), (), s32[]{:S(2)}) async-start(), calls=%async_computation.50 | async-start | bytes 61440
  2056.5 290.3 %reduce-scatter.56.cloned.1.call-start = ((), (), s32[]{:S(2)}) async-start(), calls=%async_computation.51 | async-start | bytes 61440
  2070.3 309.2 %reduce-scatter.46.cloned.1.call-start = ((), (), s32[]{:S(2)}) async-start(), calls=%async_computation.46 | async-start | bytes 40960
  2074.3 306.4 %reduce-scatter.52.cloned.1.call-start = ((), (), s32[]{:S(2)}) async-start(), calls=%async_computation.49 | async-start | bytes 61440
  2087.7 294.4 %reduce-scatter.50.cloned.1.call-start = ((), (), s32[]{:S(2)}) async-start(), calls=%async_computation.48 | async-start | bytes 61440
  2090.1 293.3 %reduce-scatter.38.cloned.1.call-start = ((), (), s32[]{:S(2)}) async-start(), calls=%async_computation.42 | async-start | bytes 491520 | tf_op jit(solution)/shard_map/reduce_scatter | solution.py:391
  2103.7 281.3 %reduce-scatter.30.cloned.1.call-start = ((), (), s32[]{:S(2)}) async-start(), calls=%async_computation.38 | async-start | bytes 491520 | tf_op jit(solution)/shard_map/reduce_scatter | solution.py:379
  2116.5 270.1 %reduce-scatter.32.cloned.1.call-start = ((), (), s32[]{:S(2)}) async-start(), calls=%async_computation.39 | async-start | bytes 491520 | tf_op jit(solution)/shard_map/reduce_scatter | solution.py:382
  2129.3 258.9 %reduce-scatter.36.cloned.1.call-start = ((), (), s32[]{:S(2)}) async-start(), calls=%async_computation.41 | async-start | bytes 737280 | tf_op jit(solution)/shard_map/reduce_scatter | solution.py:388
  2254.5 94.1 %all-to-all-start.7 = ((bf16[8,2,196608]{2,1,0:T(2,128)(2,1)}), bf16[8,2,196608]{2,1,0:T(2,128)(2,1)}, u32[]{:S(2)}, u32[]{:S(2)}) async-start(bf16[8,2,196608]{2,1,0:T(2,128)(2,1)} %reshape.890), calls=%async_computation.14 | async-start | bytes 12582912 | tf_op jit(solution)/shard_map/all_to_all | solution.py:362
  2259.3 130.5 %reduce-scatter.34.cloned.1.call-start = ((), (), s32[]{:S(2)}) async-start(), calls=%async_computation.40 | async-start | bytes 737280 | tf_op jit(solution)/shard_map/reduce_scatter | solution.py:385
  2280.1 111.4 %reduce-scatter.40.cloned.1.call-start = ((), (), s32[]{:S(2)}) async-start(), calls=%async_computation.43 | async-start | bytes 983040 | tf_op jit(solution)/shard_map/reduce_scatter | solution.py:394
  2305.9 87.3 %reduce-scatter.42.cloned.1.call-start = ((), (), s32[]{:S(2)}) async-start(), calls=%async_computation.44 | async-start | bytes 983040 | tf_op jit(solution)/shard_map/reduce_scatter | solution.py:397
  2332.4 65.1 %reduce-scatter.44.cloned.1.call-start = ((), (), s32[]{:S(2)}) async-start(), calls=%async_computation.45 | async-start | bytes 983040 | tf_op jit(solution)/shard_map/reduce_scatter | solution.py:400
  (255 other events, 2722.7 us)
Sparse Core Ops, SparseCore 0:
  10.9 58.6 all-gather.9
  72.5 57.7 all-gather.15
  133.1 63.8 all-gather.11
  199.7 62.3 all-gather.13
  264.8 56.3 all-gather.17
  324.0 69.5 all-gather.19
  396.4 68.0 all-gather.21
  467.4 68.0 all-gather.23
  2029.7 17.5 reduce-scatter.47
  2050.0 17.2 reduce-scatter.57
  2070.1 17.1 reduce-scatter.53
  2090.1 17.1 reduce-scatter.55
  2109.5 16.9 reduce-scatter.45
  2129.3 17.1 reduce-scatter.51
  2149.2 17.2 reduce-scatter.49
  2169.3 18.8 reduce-scatter.37
  2190.8 18.8 reduce-scatter.29
  2212.6 18.8 reduce-scatter.31
  2233.8 20.2 reduce-scatter.35
  2280.2 20.6 reduce-scatter.33
  2306.1 22.1 reduce-scatter.39
  2332.5 22.1 reduce-scatter.41
  2375.3 22.1 reduce-scatter.43
where the time goes:
time: 2440 us; the launch traced here: 2410 us
  local copies, waits for them, and re-layouts  1240 us (51%)
  other arithmetic  566 us (23%)
  matrix products  183 us (8%)
  blocking collectives  172 us (7%)
  waiting for transfers between devices  150 us (6%)
  starting transfers between devices  75.5 us (3%)
    unnamed x17, other arithmetic  252 us
    slice x114, local copies, waits for them, and re-layouts, backward_part(): lax.associative_scan(link, (following, d_states), reverse=True, axis=1)  244 us
    unnamed x540, local copies, waits for them, and re-layouts  225 us
    slice x104, local copies, waits for them, and re-layouts, forward_part(): reach, local = lax.associative_scan(link, (decay, drive), axis=1)  184 us
    pad x56, local copies, waits for them, and re-layouts, backward_part(): lax.associative_scan(link, (following, d_states), reverse=True, axis=1)  75.4 us
    dot_general x16, matrix products, project_back(): jnp.einsum('bte,de->btd', left, right, preferred_element_type=jnp.float32)  72.1 us
    pad x56, local copies, waits for them, and re-layouts, forward_part(): reach, local = lax.associative_scan(link, (decay, drive), axis=1)  71.7 us
    all_gather x1, blocking collectives, fetch(): lax.all_gather(conv_taps, ('seq', 'batch'), axis=1, tiled=True)  62.4 us
  transfers between devices with their start and end apart: 42, of which 7 were waited for; matrix products, arithmetic and copies ran while one was open for 63% of the time, Pallas kernels for 0%

commit v1 on v0

--- a/solution.py
+++ b/solution.py
@@ -1,6 +1,10 @@
+import functools
+
 import jax
 import jax.numpy as jnp
 from jax import lax
+from jax.experimental import pallas as pl
+from jax.experimental.pallas import tpu as pltpu
 from jax.sharding import PartitionSpec as P
 
 MICRO = 2
@@ -491,7 +495,1152 @@
     return (jnp.concatenate(block_parts, axis=0), jnp.concatenate(grad_parts, axis=0)) + summed
 
 
+F32 = jnp.float32
+BF16 = jnp.bfloat16
+W = 512
+SEGS = 8
+CHUNK = 16
+TALL = 64
+LANES = 128
+GELU_A = 0.7978845608028654
+GELU_B = 0.044715
+TAPS, CONV_BIAS, RATE_BIAS, ENTRY_BIAS, COEF, SIG = 0, 4, 5, 6, 7, 8
+
+
+def dot(left, right):
+    return lax.dot_general(left, right, (((1,), (0,)), ((), ())), preferred_element_type=F32)
+
+
+def dot_back(left, right):
+    return lax.dot_general(left, right, (((1,), (1,)), ((), ())), preferred_element_type=F32)
+
+
+def dot_outer(left, right):
+    return lax.dot_general(left, right, (((0,), (0,)), ((), ())), preferred_element_type=F32)
+
+
+def rows_at(start, count=CHUNK):
+    return pl.ds(pl.multiple_of(start, CHUNK), count)
+
+
+def gelu_both(value):
+    square = value * value
+    inside = GELU_A * value * (1.0 + GELU_B * square)
+    tanh = jnp.tanh(inside)
+    half = 0.5 + 0.5 * tanh
+    slope = half + 0.5 * value * (1.0 - tanh * tanh) * (GELU_A * (1.0 + 3.0 * GELU_B * square))
+    return value * half, slope
+
+
+def sigmoid(value):
+    return 1.0 / (1.0 + jnp.exp(-value))
+
+
+def one_less_exp(z, exp_z):
+    series = 1.0 + z * (1 / 2 + z * (1 / 6 + z * (1 / 24 + z * (1 / 120 + z * (1 / 720)))))
+    return jnp.where(z > -0.25, -z * series, 1.0 - exp_z)
+
+
+def in_row(row, width, shape):
+    return row + lax.broadcasted_iota(jnp.int32, shape, 0)
+
+
+def each_chunk(batch, width, body, carry=0):
+    per = width // CHUNK
+    for b in range(batch):
+        carry = lax.fori_loop(0, per, lambda i, c, b=b: body(b, i * CHUNK, b * width + i * CHUNK, c), carry)
+    return carry
+
+
+def each_tile(batch, width, tiles, body, carry=None):
+    carries = []
+    for t in range(tiles):
+        kept = carry
+        for b in range(batch):
+            def one(i, c, t=t, b=b):
+                return body(t, b, i * TALL, rows_at(b * width + i * TALL, TALL), slice(t * LANES, (t + 1) * LANES), c)
+            kept = lax.fori_loop(0, width // TALL, one, 0 if kept is None else kept)
+        carries.append(kept)
+    return carries
+
+
+def strided(b, width, step):
+    return pl.ds(b * width + step, SEGS, stride=width // SEGS)
+
+
+def lanes(t):
+    return slice(t * LANES, (t + 1) * LANES)
+
+
+def spread(ref, value):
+    for t in range(ref.shape[0]):
+        ref[t] = value[:, lanes(t)]
+
+
+def tiled(tokens, block, index):
+    return pl.BlockSpec((block // LANES, tokens, LANES), lambda j: (index(j), 0, 0))
+
+
+def inverse_norm(value, depth):
+    return lax.rsqrt(jnp.sum(value * value, axis=-1, keepdims=True) * (1.0 / depth) + eps)
+
+
+def fold8(value):
+    total = value[:8]
+    for i in range(8, value.shape[0], 8):
+        total = total + value[i : i + 8]
+    return total
+
+
+def branch_kernel(batch, width, x_ref, rim_ref, gain_ref, wg_ref, wi_ref, vec_ref,
+                  gate_ref, inner_ref, mixed_ref, normed_ref, ext):
+    step = pl.program_id(0)
+    tokens, depth = x_ref.shape
+    gain = gain_ref[:1]
+
+    @pl.when(step == 0)
+    def _():
+        def norm(i, _):
+            at = rows_at(i * CHUNK)
+            value = x_ref[at].astype(F32)
+            normed = (value * inverse_norm(value, depth) * gain).astype(BF16)
+            ext[at] = normed
+            normed_ref[at] = normed
+            return 0
+        lax.fori_loop(0, tokens // CHUNK, norm, 0)
+        rim = rim_ref[...].astype(F32)
+        ext[pl.ds(tokens, rim.shape[0])] = (rim * inverse_norm(rim, depth) * gain).astype(BF16)
+
+    spread(gate_ref, dot(ext[:tokens], wg_ref[...].reshape(depth, W)))
+    inner = dot(ext[...], wi_ref[...].reshape(depth, W))
+    span = width + 8
+    for b in range(batch):
+        inner_ref[b * span : b * span + 8] = inner[tokens + 8 * b : tokens + 8 * b + 8]
+        inner_ref[b * span + 8 : (b + 1) * span] = inner[b * width : (b + 1) * width]
+    for b in range(batch):
+        conv = vec_ref[CONV_BIAS : CONV_BIAS + 1]
+        for lag in range(4):
+            conv = conv + vec_ref[lag : lag + 1] * inner_ref[b * span + 8 - lag : (b + 1) * span - lag]
+        mixed_ref[b * width : (b + 1) * width] = conv.astype(BF16)
+
+
+def branch(tokens2, rim, gain, packed, vec, batch):
+    tokens, depth = tokens2.shape
+    width = tokens // batch
+    full = lambda a: pl.BlockSpec(a.shape, lambda j: (0,) * a.ndim)
+    r = vec.shape[1]
+    col = lambda rows: pl.BlockSpec((rows, W), lambda j: (0, j))
+    n = packed.shape[0]
+    rows = depth // n
+    return pl.pallas_call(
+        functools.partial(branch_kernel, batch, width),
+        grid=(r // W,),
+        in_specs=[full(tokens2), full(rim), full(gain),
+                  pl.BlockSpec((n, rows, W), lambda j: (0, GATE_AT // rows + j, 0)),
+                  pl.BlockSpec((n, rows, W), lambda j: (0, INPUT_AT // rows + j, 0)),
+                  col(vec.shape[0])],
+        out_specs=[tiled(tokens, W, lambda j: j), col(tokens + 8 * batch), col(tokens), pl.BlockSpec((tokens, depth), lambda j: (0, 0))],
+        out_shape=[jax.ShapeDtypeStruct((r // LANES, tokens, LANES), F32), jax.ShapeDtypeStruct((tokens + 8 * batch, r), F32),
+                   jax.ShapeDtypeStruct((tokens, r), BF16), jax.ShapeDtypeStruct((tokens, depth), BF16)],
+        scratch_shapes=[pltpu.VMEM((tokens + 8 * batch, depth), BF16)],
+        compiler_params=pltpu.CompilerParams(vmem_limit_bytes=50 << 20),
+    )(tokens2, rim, gain, packed, packed, vec)
+
+
+def gates_kernel(batch, width, info_ref, mixed_ref, wr_ref, we_ref, vec_ref,
+                 rate_ref, entry_ref, decay_ref, drive_ref, pseg_ref, hseg_ref, tot_ref):
+    step = pl.program_id(0)
+    r = mixed_ref.shape[1]
+    spread(rate_ref, dot(mixed_ref[...], wr_ref[...].reshape(r, W)))
+    spread(entry_ref, dot(mixed_ref[...], we_ref[...].reshape(r, W)))
+    tiles = W // LANES
+
+    def gating(t, b, spot, at, cols, _):
+        rate = sigmoid(rate_ref[t, at] + vec_ref[RATE_BIAS : RATE_BIAS + 1, cols])
+        entry = sigmoid(entry_ref[t, at] + vec_ref[ENTRY_BIAS : ENTRY_BIAS + 1, cols])
+        log_decay = vec_ref[COEF : COEF + 1, cols] * rate
+        z = 2.0 * log_decay
+        root = jnp.sqrt(one_less_exp(z, jnp.exp(z)))
+        valid = in_row(spot, width, rate.shape) < info_ref[b]
+        rate_ref[t, at] = rate
+        entry_ref[t, at] = entry
+        decay_ref[t, at] = jnp.where(valid, jnp.exp(log_decay), 1.0)
+        mixed = mixed_ref[at, pl.ds(pl.multiple_of(step * W + t * LANES, LANES), LANES)].astype(F32)
+        drive_ref[t, at] = jnp.where(valid, root * entry * mixed, 0.0)
+        return 0
+
+    each_tile(batch, width, tiles, gating)
+    tot_ref[...] = jnp.zeros_like(tot_ref)
+    for t in range(tiles):
+        cols = lanes(t)
+        for b in range(batch):
+            prod = jnp.ones((SEGS, LANES), F32)
+            state = jnp.zeros((SEGS, LANES), F32)
+            for s in range(width // SEGS):
+                at = strided(b, width, s)
+                a = decay_ref[t, at]
+                state = a * state + drive_ref[t, at]
+                prod = prod * a
+            pseg_ref[b * SEGS : (b + 1) * SEGS, cols] = prod
+            hseg_ref[b * SEGS : (b + 1) * SEGS, cols] = state
+            whole, end = prod[:1], state[:1]
+            for i in range(1, SEGS):
+                whole = whole * prod[i : i + 1]
+                end = prod[i : i + 1] * end + state[i : i + 1]
+            tot_ref[b : b + 1, cols] = whole
+            tot_ref[batch + b : batch + b + 1, cols] = end
+
+
+def gates(info, mixed, packed, vec, batch):
+    tokens, r = mixed.shape
+    width = tokens // batch
+    n = packed.shape[0]
+    rows = r // n
+    col = lambda count: pl.BlockSpec((count, W), lambda j: (0, j))
+    big = jax.ShapeDtypeStruct((r // LANES, tokens, LANES), F32)
+    seg = jax.ShapeDtypeStruct((batch * SEGS, r), F32)
+    return pl.pallas_call(
+        functools.partial(gates_kernel, batch, width),
+        grid=(r // W,),
+        in_specs=[pl.BlockSpec(memory_space=pltpu.SMEM), pl.BlockSpec((tokens, r), lambda j: (0, 0)),
+                  pl.BlockSpec((n, rows, W), lambda j: (0, RATE_AT // rows + j, 0)),
+                  pl.BlockSpec((n, rows, W), lambda j: (0, ENTRY_AT // rows + j, 0)),
+                  col(vec.shape[0])],
+        out_specs=[tiled(tokens, W, lambda j: j)] * 4 + [col(batch * SEGS)] * 2 + [col(8)],
+        out_shape=[big] * 4 + [seg] * 2 + [jax.ShapeDtypeStruct((8, r), F32)],
+        compiler_params=pltpu.CompilerParams(vmem_limit_bytes=50 << 20),
+    )(info, mixed, packed, packed, vec)
+
+
+def exchange_kernel(n, x_ref, o_ref, send, recv, own):
+    me, z = lax.axis_index("seq"), lax.axis_index("batch")
+    bar = pltpu.get_barrier_semaphore()
+    for k in range(1, n):
+        pl.semaphore_signal(bar, inc=1, device_id=(lax.rem(me + k, n), z), device_id_type=MESH)
+    pl.semaphore_wait(bar, n - 1)
+    mine = pltpu.make_async_copy(x_ref, o_ref.at[me], own)
+    mine.start()
+    copies = []
+    for k in range(1, n):
+        copies.append(pltpu.make_async_remote_copy(
+            x_ref, o_ref.at[me], send.at[k], recv.at[k],
+            device_id=(lax.rem(me + k, n), z), device_id_type=MESH))
+    for copy in copies:
+        copy.start()
+    mine.wait()
+    for copy in copies:
+        copy.wait()
+
+
+def exchange(value, n, ident):
+    D = pltpu.SemaphoreType.DMA
+    return pl.pallas_call(
+        functools.partial(exchange_kernel, n),
+        out_shape=jax.ShapeDtypeStruct((n,) + value.shape, value.dtype),
+        in_specs=[pl.BlockSpec(memory_space=pltpu.VMEM)],
+        out_specs=pl.BlockSpec(memory_space=pltpu.VMEM),
+        scratch_shapes=[D((n,)), D((n,)), D],
+        compiler_params=pltpu.CompilerParams(collective_id=ident, has_side_effects=True),
+    )(value)
+
+
+def states_kernel(batch, width, n_seq, info_ref, decay_ref, drive_ref, gate_ref, pseg_ref, hseg_ref, all_ref,
+                  x_ref, wo_ref, gain_ref, states_ref, sstart_ref, gated_ref, first_ref, normed_ref):
+    step = pl.program_id(0)
+    tokens, depth = x_ref.shape
+    r = gated_ref.shape[1]
+    parts = r // W
+
+    @pl.when(step < parts)
+    def _():
+        me = info_ref[batch]
+        for b in range(batch):
+            start = jnp.zeros((1, W), F32)
+            for k in range(n_seq):
+                new = all_ref[k, b : b + 1] * start + all_ref[k, batch + b : batch + b + 1]
+                start = jnp.where(k < me, new, start)
+            for i in range(SEGS):
+                at = b * SEGS + i
+                sstart_ref[at : at + 1] = start
+                start = pseg_ref[at : at + 1] * start + hseg_ref[at : at + 1]
+            for t in range(W // LANES):
+                state = sstart_ref[b * SEGS : (b + 1) * SEGS, lanes(t)]
+                for s in range(width // SEGS):
+                    at = strided(b, width, s)
+                    state = decay_ref[t, at] * state + drive_ref[t, at]
+                    states_ref[t, at] = state
+        j = jnp.minimum(step, parts - 1)
+
+        def gating(t, b, spot, at, cols, _):
+            gate = gelu_both(gate_ref[t, at])[0]
+            gated_ref[at, pl.ds(pl.multiple_of(j * W + t * LANES, LANES), LANES)] = (states_ref[t, at] * gate).astype(BF16)
+            return 0
+        each_tile(batch, width, W // LANES, gating)
+
+    for half in range(depth // W):
+        @pl.when(step == parts + half)
+        def _():
+            cols = slice(half * W, (half + 1) * W)
+            first_ref[:, cols] = x_ref[:, cols].astype(F32) + dot(gated_ref[...], wo_ref[...].reshape(r, W))
+
+    @pl.when(step == pl.num_programs(0) - 1)
+    def _():
+        def norm(i, _):
+            at = rows_at(i * CHUNK)
+            value = first_ref[at]
+            normed_ref[at] = (value * inverse_norm(value, depth) * gain_ref[:1]).astype(BF16)
+            return 0
+        lax.fori_loop(0, tokens // CHUNK, norm, 0)
+
+
+def states_and_first(info, decay, drive, gate_pre, pseg, hseg, everyone, tokens2, packed, gain, batch):
+    tokens, depth = tokens2.shape
+    r = pseg.shape[1]
+    width = tokens // batch
+    n = packed.shape[0]
+    rows = r // n
+    parts = r // W
+    col = lambda count: pl.BlockSpec((count, W), lambda j: (0, jnp.minimum(j, parts - 1)))
+    full = lambda shape: pl.BlockSpec(shape, lambda j: (0,) * len(shape))
+    return pl.pallas_call(
+        functools.partial(states_kernel, batch, width, everyone.shape[0]),
+        grid=(parts + depth // W,),
+        in_specs=[pl.BlockSpec(memory_space=pltpu.SMEM)] + [tiled(tokens, W, lambda j: jnp.minimum(j, parts - 1))] * 3 + [
+                  col(batch * SEGS), col(batch * SEGS),
+                  pl.BlockSpec((everyone.shape[0], 8, W), lambda j: (0, 0, jnp.minimum(j, parts - 1))),
+                  full(tokens2.shape),
+                  pl.BlockSpec((n, rows, W), lambda j: (0, OUT_AT // rows + jnp.maximum(j - parts, 0), 0)),
+                  full(gain.shape)],
+        out_specs=[tiled(tokens, W, lambda j: jnp.minimum(j, parts - 1)), col(batch * SEGS), full((tokens, r)),
+                   full((tokens, depth)), full((tokens, depth))],
+        out_shape=[jax.ShapeDtypeStruct((r // LANES, tokens, LANES), F32), jax.ShapeDtypeStruct((batch * SEGS, r), F32),
+                   jax.ShapeDtypeStruct((tokens, r), BF16), jax.ShapeDtypeStruct((tokens, depth), F32),
+                   jax.ShapeDtypeStruct((tokens, depth), BF16)],
+        compiler_params=pltpu.CompilerParams(vmem_limit_bytes=50 << 20),
+    )(info, decay, drive, gate_pre, pseg, hseg, everyone, tokens2, packed, gain)
+
+
+def put(stage, sem, slot, dst, value, used):
+    copy = pltpu.make_async_copy(stage.at[slot], dst, sem.at[slot])
+    if used is True:
+        copy.wait()
+    elif used is not False:
+        pl.when(used)(copy.wait)
+    stage[slot] = value
+    copy.start()
+
+
+def ffn_kernel(batch, width, info_ref, first_ref, normed_ref, cot_ref, gain_ref, wg_ref, wu_ref, wd_ref,
+               out_ref, dfirst_ref, dlow_ref, ggain_ref, grad_ref,
+               low, dh, hid, acc, dn, up_s, mix_s, du, dm, nt, ltr, stage, dstage, sem, dsem):
+    step = pl.program_id(0)
+    tokens, depth = first_ref.shape
+    n = grad_ref.shape[0]
+    f = hid.shape[1]
+    wide = wd_ref.shape[0] * wd_ref.shape[1] // 2
+    nd, nw = f // wide, f // W
+    rows = depth // n
+    drows = wd_ref.shape[1] // 2
+
+    @pl.when(step == 0)
+    def _():
+        def masked(b, spot, row, _):
+            at = rows_at(row)
+            value = cot_ref[at]
+            valid = in_row(spot, width, value.shape) < info_ref[b]
+            low[at] = jnp.where(valid, value.astype(F32), 0.0).astype(BF16)
+            return 0
+        each_chunk(batch, width, masked)
+
+    @pl.when(step < nd)
+    def _():
+        here = pl.ds(pl.multiple_of(jnp.minimum(step, nd - 1) * wide, wide), wide)
+        total = dot_back(low[:, :W], wd_ref[:, :drows].reshape(wide, W))
+        dh[:, here] = total + dot_back(low[:, W:], wd_ref[:, drows:].reshape(wide, W))
+
+    @pl.when(jnp.logical_and(step >= nd, step < nd + nw))
+    def _():
+        j = step - nd
+        here = pl.ds(pl.multiple_of(j * W, W), W)
+        wg = wg_ref[...].reshape(depth, W)
+        wu = wu_ref[...].reshape(depth, W)
+        up_s[...] = dot(normed_ref[...], wg)
+        mix_s[...] = dot(normed_ref[...], wu)
+
+        def gating(i, _):
+            at = rows_at(i * CHUNK)
+            gate, slope = gelu_both(up_s[at])
+            mix, d = mix_s[at], dh[at, here]
+            hid[at, here] = (gate * mix).astype(BF16)
+            du[at] = (d * mix * slope).astype(BF16)
+            dm[at] = (d * gate).astype(BF16)
+            return 0
+        lax.fori_loop(0, tokens // CHUNK, gating, 0)
+        more = dot_back(du[...], wg) + dot_back(dm[...], wu)
+
+        @pl.when(j == 0)
+        def _():
+            dn[...] = more
+
+        @pl.when(j > 0)
+        def _():
+            dn[...] += more
+        for which, low_grad in ((0, du), (1, dm)):
+            value = dot_outer(normed_ref[...], low_grad[...]).astype(BF16).reshape(n, rows, W)
+            dst = grad_ref.at[:, pl.ds(pl.multiple_of(which * nw * rows + j * rows, rows), rows)]
+            put(stage, sem, which, dst, value, j > 0)
+
+    @pl.when(step >= nd + nw)
+    def _():
+        k = step - nd - nw
+        here = pl.ds(pl.multiple_of(k * wide, wide), wide)
+        block = hid[:, here]
+        for half in range(2):
+            cols = slice(half * W, (half + 1) * W)
+            more = dot(block, wd_ref[:, half * drows : (half + 1) * drows].reshape(wide, W))
+
+            @pl.when(k == 0)
+            def _():
+                acc[:, cols] = more
+
+            @pl.when(k > 0)
+            def _():
+                acc[:, cols] += more
+            value = dot_outer(block, low[:, cols]).astype(BF16).reshape(wide // drows, drows, W)
+            dst = grad_ref.at[pl.ds(k * (wide // drows), wide // drows),
+                              pl.ds(2 * nw * rows + half * drows, drows)]
+            put(dstage, dsem, half, dst, value, k > 0)
+
+    @pl.when(step == pl.num_programs(0) - 1)
+    def _():
+        def finish(b, spot, row, total):
+            at = rows_at(row)
+            first, cot = first_ref[at], low[at].astype(F32)
+            valid = in_row(spot, width, first.shape) < info_ref[b]
+            out_ref[at] = jnp.where(valid, first + acc[at], 0.0)
+            grad = dn[at]
+            scale = inverse_norm(first, depth)
+            weighted = grad * gain_ref[:1]
+            spread = jnp.sum(weighted * first, axis=-1, keepdims=True) * (1.0 / depth)
+            back = cot + scale * weighted - first * (scale * scale * scale * spread)
+            dfirst_ref[at] = back
+            dlow_ref[at] = back.astype(BF16)
+            return total + fold8(grad * first * scale)
+        total = each_chunk(batch, width, finish, jnp.zeros((8, depth), F32))
+        ggain_ref[...] = total
+        for which in range(2):
+            pltpu.make_async_copy(stage.at[which], grad_ref.at[:, pl.ds(0, rows)], sem.at[which]).wait()
+            pltpu.make_async_copy(dstage.at[which], grad_ref.at[pl.ds(0, wide // drows), pl.ds(0, drows)], dsem.at[which]).wait()
+
+
+def feed_forward(info, first, normed_two, cot, gain, packed, f, batch):
+    tokens, depth = first.shape
+    width = tokens // batch
+    n = packed.shape[0]
+    rows, drows = depth // n, f // n
+    group = 8
+    wide = group * drows
+    nd, nw = f // wide, f // W
+    full = lambda shape: pl.BlockSpec(shape, lambda j: (0,) * len(shape))
+    clamp = lambda j, low, count: jnp.clip(j - low, 0, count - 1)
+    down = FFN_DOWN_AT // (2 * drows)
+
+    def down_block(j):
+        return (jnp.where(j < nd, jnp.minimum(j, nd - 1), clamp(j, nd + nw, nd)), down, 0)
+    vm = pltpu.VMEM
+    return pl.pallas_call(
+        functools.partial(ffn_kernel, batch, width),
+        grid=(nd + nw + nd,),
+        in_specs=[pl.BlockSpec(memory_space=pltpu.SMEM), full(first.shape), full(normed_two.shape), full(cot.shape),
+                  full(gain.shape),
+                  pl.BlockSpec((n, rows, W), lambda j: (0, FFN_GATE_AT // rows + clamp(j, nd, nw), 0)),
+                  pl.BlockSpec((n, rows, W), lambda j: (0, FFN_UP_AT // rows + clamp(j, nd, nw), 0)),
+                  pl.BlockSpec((group, 2 * drows, W), down_block)],
+        out_specs=[full((tokens, depth))] * 3 + [full((8, depth)), pl.BlockSpec(memory_space=pl.ANY)],
+        out_shape=[jax.ShapeDtypeStruct((tokens, depth), F32), jax.ShapeDtypeStruct((tokens, depth), F32),
+                   jax.ShapeDtypeStruct((tokens, depth), BF16), jax.ShapeDtypeStruct((8, depth), F32),
+                   jax.ShapeDtypeStruct((n, 2 * nw * rows + 2 * drows, W), BF16)],
+        scratch_shapes=[vm((tokens, depth), BF16), vm((tokens, f), F32), vm((tokens, f), BF16), vm((tokens, depth), F32),
+                        vm((tokens, depth), F32), vm((tokens, W), F32), vm((tokens, W), F32), vm((tokens, W), BF16),
+                        vm((tokens, W), BF16), vm((8, 128), BF16), vm((8, 128), BF16),
+                        vm((2, n, rows, W), BF16), vm((2, group, drows, W), BF16),
+                        pltpu.SemaphoreType.DMA((2,)), pltpu.SemaphoreType.DMA((2,))],
+        compiler_params=pltpu.CompilerParams(vmem_limit_bytes=60 << 20),
+    )(info, first, normed_two, cot, gain, packed, packed, packed)
+
+
+def unproject_kernel(batch, width, dlow_ref, wo_ref, gated_ref, gate_ref, states_ref, decay_ref, pseg_ref,
+                     dstates_ref, dgate_ref, gseg_ref, gtot_ref, grad_ref, stage, sem):
+    step = pl.program_id(0)
+    tokens, depth = dlow_ref.shape
+    orows = wo_ref.shape[1] // 2
+    group = wo_ref.shape[0]
+    wide = group * orows
+    dg = dot_back(dlow_ref[:, :W], wo_ref[:, :orows].reshape(wide, W))
+    spread(dstates_ref, dg + dot_back(dlow_ref[:, W:], wo_ref[:, orows:].reshape(wide, W)))
+
+    def gating(t, b, spot, at, cols, _):
+        gate, slope = gelu_both(gate_ref[t, at])
+        d = dstates_ref[t, at]
+        dstates_ref[t, at] = d * gate
+        dgate_ref[at, cols] = (d * states_ref[t, at] * slope).astype(BF16)
+        return 0
+    each_tile(batch, width, wide // LANES, gating)
+    for half in range(2):
+        value = dot_outer(gated_ref[...], dlow_ref[:, half * W : (half + 1) * W]).astype(BF16)
+        dst = grad_ref.at[pl.ds(step * group, group), pl.ds(OUT_AT + half * orows, orows)]
+        put(stage, sem, half, dst, value.reshape(group, orows, W), step > 0)
+    gtot_ref[...] = jnp.zeros_like(gtot_ref)
+    for t in range(wide // LANES):
+        cols = lanes(t)
+        for b in range(batch):
+            grad = jnp.zeros((SEGS, LANES), F32)
+            for s in reversed(range(width // SEGS)):
+                at = strided(b, width, s)
+                grad = decay_ref[t, at] * (dstates_ref[t, at] + grad)
+            gseg_ref[b * SEGS : (b + 1) * SEGS, cols] = grad
+            whole = grad[SEGS - 1 :]
+            for i in reversed(range(SEGS - 1)):
+                whole = grad[i : i + 1] + pseg_ref[b * SEGS + i : b * SEGS + i + 1, cols] * whole
+            gtot_ref[b : b + 1, cols] = whole
+
+    @pl.when(step == pl.num_programs(0) - 1)
+    def _():
+        for half in range(2):
+            pltpu.make_async_copy(stage.at[half], grad_ref.at[pl.ds(0, group), pl.ds(OUT_AT, orows)], sem.at[half]).wait()
+
+
+def unproject(dlow, packed, gated, gate_pre, states, decay, pseg, batch):
+    tokens, r = gated.shape
+    depth = dlow.shape[1]
+    width = tokens // batch
+    n = packed.shape[0]
+    orows = r // n
+    group = n // 2
+    wide = group * orows
+    col = lambda count: pl.BlockSpec((count, wide), lambda j: (0, j))
+    return pl.pallas_call(
+        functools.partial(unproject_kernel, batch, width),
+        grid=(n // group,),
+        in_specs=[pl.BlockSpec((tokens, depth), lambda j: (0, 0)),
+                  pl.BlockSpec((group, 2 * orows, W), lambda j: (j, OUT_AT // (2 * orows), 0)),
+                  col(tokens)] + [tiled(tokens, wide, lambda j: j)] * 3 + [col(batch * SEGS)],
+        out_specs=[tiled(tokens, wide, lambda j: j), col(tokens), col(batch * SEGS), col(8), pl.BlockSpec(memory_space=pl.ANY)],
+        out_shape=[jax.ShapeDtypeStruct((r // LANES, tokens, LANES), F32), jax.ShapeDtypeStruct((tokens, r), BF16),
+                   jax.ShapeDtypeStruct((batch * SEGS, r), F32), jax.ShapeDtypeStruct((8, r), F32),
+                   jax.ShapeDtypeStruct((n, REC_ROWS, W), BF16)],
+        scratch_shapes=[pltpu.VMEM((2, group, orows, W), BF16),
+                        pltpu.SemaphoreType.DMA((2,))],
+        compiler_params=pltpu.CompilerParams(vmem_limit_bytes=60 << 20),
+    )(dlow, packed, gated, gate_pre, states, decay, pseg)
+
+
+def recur_kernel(batch, width, n_seq, info_ref, mixed_ref, decay_ref, dstates_ref, states_ref, rate_ref, entry_ref,
+                 pseg_ref, gseg_ref, sstart_ref, pall_ref, gall_ref, vec_ref, wr_ref, we_ref, _,
+                 dmixed_ref, sums_ref, grad_ref, carried, across, gstart, rl, el, direct, stage, sem):
+    step = pl.program_id(0)
+    tokens, r = mixed_ref.shape
+    n = grad_ref.shape[0]
+    rows = r // n
+    parts = r // W
+    group = wr_ref.shape[0]
+    wide = group * rows
+
+    @pl.when(step < parts)
+    def _():
+        me = info_ref[batch]
+        for b in range(batch):
+            grad = jnp.zeros((1, W), F32)
+            for k in reversed(range(n_seq)):
+                new = pall_ref[k, b : b + 1] * grad + gall_ref[k, b : b + 1]
+                grad = jnp.where(k > me, new, grad)
+            for i in reversed(range(SEGS)):
+                at = b * SEGS + i
+                gstart[i : i + 1] = grad
+                grad = pseg_ref[at : at + 1] * grad + gseg_ref[at : at + 1]
+            for t in range(W // LANES):
+                grad = gstart[:, lanes(t)]
+                for s in reversed(range(width // SEGS)):
+                    at = strided(b, width, s)
+                    total = dstates_ref[t, at] + grad
+                    carried[t, at] = total
+                    grad = decay_ref[t, at] * total
+                    before = states_ref[t, strided(b, width, s - 1)] if s else sstart_ref[b * SEGS : (b + 1) * SEGS, lanes(t)]
+                    across[t, at] = grad * before
+        j = jnp.minimum(step, parts - 1)
+        here = pl.ds(pl.multiple_of(j * W, W), W)
+
+        def gating(t, b, spot, at, cols, sums):
+            tile = pl.ds(pl.multiple_of(j * W + t * LANES, LANES), LANES)
+            coef = vec_ref[COEF : COEF + 1, cols]
+            rate, entry = rate_ref[t, at], entry_ref[t, at]
+            valid = in_row(spot, width, rate.shape) < info_ref[b]
+            grad = jnp.where(valid, carried[t, at], 0.0)
+            z = 2.0 * coef * rate
+            exp_z = jnp.exp(z)
+            under = one_less_exp(z, exp_z)
+            inverse = lax.rsqrt(under)
+            root = under * inverse
+            mixed = mixed_ref[at, tile].astype(F32)
+            part = grad * entry
+            d_log = jnp.where(valid, across[t, at], 0.0) - part * mixed * exp_z * inverse
+            d_rate = coef * d_log * rate * (1.0 - rate)
+            straight = part * root
+            d_entry = straight * mixed * (1.0 - entry)
+            direct[at, tile] = straight
+            rl[at, tile] = d_rate.astype(BF16)
+            el[at, tile] = d_entry.astype(BF16)
+            return (sums[0] + fold8(d_log * rate), sums[1] + fold8(d_rate), sums[2] + fold8(d_entry))
+        zero = jnp.zeros((8, LANES), F32)
+        sums = each_tile(batch, width, W // LANES, gating, (zero, zero, zero))
+        sums_ref[...] = jnp.zeros_like(sums_ref)
+        for t, kept in enumerate(sums):
+            for line in range(3):
+                factor = 8.0 * vec_ref[SIG : SIG + 1, lanes(t)] if line == 0 else 1.0
+                sums_ref[line : line + 1, lanes(t)] = factor * jnp.sum(kept[line], axis=0, keepdims=True)
+        for which, low_grad, base in ((0, rl, RATE_AT), (1, el, ENTRY_AT)):
+            value = dot_outer(mixed_ref[...], low_grad[:, here]).astype(BF16).reshape(n, rows, W)
+            dst = grad_ref.at[:, pl.ds(pl.multiple_of(base + j * rows, 16), rows)]
+            put(stage, sem, which, dst, value, step > 0)
+
+    @pl.when(step >= parts)
+    def _():
+        k = jnp.maximum(step - parts, 0)
+        here = pl.ds(pl.multiple_of(k * wide, wide), wide)
+        total = direct[:, here]
+        for p in range(parts):
+            cols = slice(p * W, (p + 1) * W)
+            total = total + dot_back(rl[:, cols], wr_ref[:, p * rows : (p + 1) * rows].reshape(wide, W))
+            total = total + dot_back(el[:, cols], we_ref[:, p * rows : (p + 1) * rows].reshape(wide, W))
+        dmixed_ref[...] = total
+
+    @pl.when(step == pl.num_programs(0) - 1)
+    def _():
+        for which in range(2):
+            pltpu.make_async_copy(stage.at[which], grad_ref.at[:, pl.ds(0, rows)], sem.at[which]).wait()
+
+
+def recur_back(info, mixed, decay, dstates, states, rate, entry, pseg, gseg, sstart, pall, gall, vec, packed, grad, batch):
+    tokens, r = mixed.shape
+    width = tokens // batch
+    n = packed.shape[0]
+    rows = r // n
+    parts = r // W
+    group = n // 2
+    wide = group * rows
+    n_seq = pall.shape[0]
+    col = lambda count: pl.BlockSpec((count, W), lambda j: (0, jnp.minimum(j, parts - 1)))
+    over = pl.BlockSpec((n_seq, 8, W), lambda j: (0, 0, jnp.minimum(j, parts - 1)))
+    later = lambda j: jnp.maximum(j - parts, 0)
+    vm = pltpu.VMEM
+    return pl.pallas_call(
+        functools.partial(recur_kernel, batch, width, n_seq),
+        grid=(parts + n // group,),
+        in_specs=[pl.BlockSpec(memory_space=pltpu.SMEM), pl.BlockSpec((tokens, r), lambda j: (0, 0))]
+        + [tiled(tokens, W, lambda j: jnp.minimum(j, parts - 1))] * 5 + [col(batch * SEGS)] * 3 + [over, over, col(vec.shape[0]),
+            pl.BlockSpec((group, parts * rows, W), lambda j: (later(j), RATE_AT // (parts * rows), 0)),
+            pl.BlockSpec((group, parts * rows, W), lambda j: (later(j), ENTRY_AT // (parts * rows), 0)),
+            pl.BlockSpec(memory_space=pl.ANY)],
+        out_specs=[pl.BlockSpec((tokens, wide), lambda j: (0, later(j))), col(8), pl.BlockSpec(memory_space=pl.ANY)],
+        out_shape=[jax.ShapeDtypeStruct((tokens, r), F32), jax.ShapeDtypeStruct((8, r), F32),
+                   jax.ShapeDtypeStruct(grad.shape, grad.dtype)],
+        input_output_aliases={15: 2},
+        scratch_shapes=[vm((W // LANES, tokens, LANES), F32), vm((W // LANES, tokens, LANES), F32), vm((SEGS, W), F32), vm((tokens, r), BF16),
+                        vm((tokens, r), BF16), vm((tokens, r), F32), vm((2, n, rows, W), BF16),
+                        pltpu.SemaphoreType.DMA((2,))],
+        compiler_params=pltpu.CompilerParams(vmem_limit_bytes=60 << 20),
+    )(info, mixed, decay, dstates, states, rate, entry, pseg, gseg, sstart, pall, gall, vec, packed, packed, grad)
+
+
+def entry_kernel(batch, width, dmixed_ref, rim_ref, inner_ref, dgate_ref, normed_ref, wg_ref, wi_ref, vec_ref,
+                 x_ref, dfirst_ref, gain_ref, _, sums_ref, token_ref, ggain_ref, grad_ref, ext, di, dn, stage, sem):
+    step = pl.program_id(0)
+    tokens, depth = x_ref.shape
+    n = grad_ref.shape[0]
+    rows = depth // n
+    span = width + 8
+    sums_ref[...] = jnp.zeros_like(sums_ref)
+    for b in range(batch):
+        ext[b * span : b * span + width] = dmixed_ref[b * width : (b + 1) * width]
+        ext[b * span + width : (b + 1) * span] = rim_ref[b * 8 : (b + 1) * 8]
+    for b in range(batch):
+        total = jnp.zeros((width, W), F32)
+        for lag in range(4):
+            total = total + vec_ref[lag : lag + 1] * ext[b * span + lag : b * span + lag + width]
+        di[b * width : (b + 1) * width] = total.astype(BF16)
+        d_mixed = dmixed_ref[b * width : (b + 1) * width]
+        for lag in range(4):
+            product = d_mixed * inner_ref[b * span + 8 - lag : (b + 1) * span - lag]
+            sums_ref[lag : lag + 1] += jnp.sum(product, axis=0, keepdims=True)
+        sums_ref[4:5] += jnp.sum(d_mixed, axis=0, keepdims=True)
+    wg = wg_ref[...].reshape(depth, W)
+    wi = wi_ref[...].reshape(depth, W)
+    more = dot_back(dgate_ref[...], wg) + dot_back(di[...], wi)
+
+    @pl.when(step == 0)
+    def _():
+        dn[...] = more
+
+    @pl.when(step > 0)
+    def _():
+        dn[...] += more
+    for which, low_grad, base in ((0, dgate_ref, GATE_AT), (1, di, INPUT_AT)):
+        value = dot_outer(normed_ref[...], low_grad[...]).astype(BF16).reshape(n, rows, W)
+        dst = grad_ref.at[:, pl.ds(pl.multiple_of(base + step * rows, 16), rows)]
+        put(stage, sem, which, dst, value, step > 0)
+
+    @pl.when(step == pl.num_programs(0) - 1)
+    def _():
+        def finish(i, total):
+            at = rows_at(i * CHUNK)
+            value, grad = x_ref[at].astype(F32), dn[at]
+            scale = inverse_norm(value, depth)
+            weighted = grad * gain_ref[:1]
+            spread = jnp.sum(weighted * value, axis=-1, keepdims=True) * (1.0 / depth)
+            token_ref[at] = dfirst_ref[at] + scale * weighted - value * (scale * scale * scale * spread)
+            return total + fold8(grad * value * scale)
+        ggain_ref[...] = lax.fori_loop(0, tokens // CHUNK, finish, jnp.zeros((8, depth), F32))
+        for which in range(2):
+            pltpu.make_async_copy(stage.at[which], grad_ref.at[:, pl.ds(0, rows)], sem.at[which]).wait()
+
+
+def entry_back(dmixed, rim, inner, dgate, normed, packed, vec, tokens2, dfirst, gain, grad, batch):
+    tokens, r = dmixed.shape
+    depth = tokens2.shape[1]
+    width = tokens // batch
+    n = packed.shape[0]
+    rows = depth // n
+    col = lambda count: pl.BlockSpec((count, W), lambda j: (0, j))
+    full = lambda shape: pl.BlockSpec(shape, lambda j: (0,) * len(shape))
+    vm = pltpu.VMEM
+    return pl.pallas_call(
+        functools.partial(entry_kernel, batch, width),
+        grid=(r // W,),
+        in_specs=[col(tokens), col(rim.shape[0]), col(inner.shape[0]), col(tokens), full(normed.shape),
+                  pl.BlockSpec((n, rows, W), lambda j: (0, GATE_AT // rows + j, 0)),
+                  pl.BlockSpec((n, rows, W), lambda j: (0, INPUT_AT // rows + j, 0)),
+                  col(vec.shape[0]), full(tokens2.shape), full(dfirst.shape), full(gain.shape),
+                  pl.BlockSpec(memory_space=pl.ANY)],
+        out_specs=[col(8), full((tokens, depth)), full((8, depth)), pl.BlockSpec(memory_space=pl.ANY)],
+        out_shape=[jax.ShapeDtypeStruct((8, r), F32), jax.ShapeDtypeStruct((tokens, depth), F32),
+                   jax.ShapeDtypeStruct((8, depth), F32), jax.ShapeDtypeStruct(grad.shape, grad.dtype)],
+        input_output_aliases={11: 3},
+        scratch_shapes=[vm((tokens + 8 * batch, W), F32), vm((tokens, W), BF16), vm((tokens, depth), F32),
+                        vm((2, n, rows, W), BF16), pltpu.SemaphoreType.DMA((2,))],
+        compiler_params=pltpu.CompilerParams(vmem_limit_bytes=60 << 20),
+    )(dmixed, rim, inner, dgate, normed, packed, packed, vec, tokens2, dfirst, gain, grad)
+
+
+MESH = pl.DeviceIdType.MESH
+ROUTES = (("z", "x", "y"), ("z", "y", "x"), ("x", "z", "y"), ("y", "z", "x"))
+ZN = 4
+STG = 4
+SEM = pltpu.SemaphoreType.DMA
+
+
+def place():
+    s = lax.axis_index("seq")
+    return lax.rem(s, 2), lax.rem(lax.div(s, 2), 2), lax.div(s, 4), lax.axis_index("batch")
+
+
+def flip(value, by):
+    return 1 - value if by else value
+
+
+def seq_of(y, x, c):
+    return (y * 2 + x) * 2 + c
+
+
+def far(z, j):
+    if j == ZN - 1:
+        return z
+    found = None
+    for here in range(ZN):
+        others = sorted((q for q in range(ZN) if q != here), key=lambda q: (-abs(q - here), q))
+        found = jnp.int32(others[j]) if found is None else jnp.where(z == here, others[j], found)
+    return found
+
+
+class Links:
+    def __init__(self):
+        self.c, self.x, self.y, self.z = c, x, y, z = place()
+        self.beside = {
+            "x": (seq_of(y, 1 - x, c), z),
+            "y": (seq_of(1 - y, x, c), z),
+            "up": (seq_of(y, x, c), z + 1),
+            "dn": (seq_of(y, x, c), z - 1),
+            "core": (seq_of(y, x, 1 - c), z),
+        }
+        self.spots = [far(z, j) for j in range(ZN)]
+        self.above, self.below = z < ZN - 1, z > 0
+
+    def greet(self):
+        bar = pltpu.get_barrier_semaphore()
+
+        def signal(d):
+            pl.semaphore_signal(bar, inc=1, device_id=self.beside[d], device_id_type=MESH)
+        for d in ("x", "y", "core"):
+            signal(d)
+        pl.when(self.above)(lambda: signal("up"))
+        pl.when(self.below)(lambda: signal("dn"))
+        pl.semaphore_wait(bar, 3 + self.above.astype(jnp.int32) + self.below.astype(jnp.int32))
+
+    def slot(self, dx, dy, z, core):
+        return seq_of(flip(self.y, dy), flip(self.x, dx), core) * ZN + z
+
+    def copy(self, src, dst, send, recv, d):
+        return pltpu.make_async_remote_copy(src, dst, send, recv, device_id=self.beside[d], device_id_type=MESH)
+
+
+def onward(order, dx, dy, same):
+    off = {"x": dx, "y": dy, "z": 0 if same else 1}
+    return [
+        d for i, d in enumerate(order)
+        if not any(off[e] for e in order[i + 1 :]) and not (d != "z" and off[d])
+    ]
+
+
+def arrival(order, dx, dy, same):
+    off = {"x": dx, "y": dy, "z": 0 if same else 1}
+    return [d for d in order if off[d]][-1]
+
+
+def blocks(parts):
+    found = [
+        (dx + dy + ZN - 1 - j, r, dx, dy, j)
+        for dx in range(2) for dy in range(2) for j in range(ZN) for r in range(len(parts))
+    ]
+    return found
+
+
+class Gather:
+    def __init__(self, parts, ins, outs, send, recv, csend, crecv, lsem):
+        self.parts, self.ins, self.outs = parts, ins, outs
+        self.send, self.recv, self.csend, self.crecv, self.lsem = send, recv, csend, crecv, lsem
+        self.links = Links()
+        self.events = sorted(blocks(parts), key=lambda e: e[0])
+
+    @staticmethod
+    def scratch(parts):
+        n = len(parts)
+        return [SEM((n, 4, 4, ZN)), SEM((n, 4, ZN)), SEM((n, 4, ZN)), SEM((n, 4, ZN)), SEM((n,))]
+
+    def window(self, r):
+        return pl.ds(self.parts[r][2], self.parts[r][3])
+
+    def dst(self, r, dx, dy, zs):
+        return self.outs[self.parts[r][1]].at[self.links.slot(dx, dy, zs, self.links.c), self.window(r)]
+
+    def src(self, r, dx, dy, zs, own):
+        return self.ins[self.parts[r][0]].at[self.window(r)] if own else self.dst(r, dx, dy, zs)
+
+    def hop(self, r, dx, dy, zs, d, own):
+        to = (1 if d == "x" else dx) * 2 + (1 if d == "y" else dy)
+        which = ("x", "y", "up", "dn").index(d)
+        return self.links.copy(self.src(r, dx, dy, zs, own), self.dst(r, dx, dy, zs),
+                               self.send.at[r, which, dx * 2 + dy, zs], self.recv.at[r, to, zs], d)
+
+    def across(self, r, dx, dy, zs, own):
+        return self.links.copy(self.src(r, dx, dy, zs, own), self.dst(r, dx, dy, zs),
+                               self.csend.at[r, dx * 2 + dy, zs], self.crecv.at[r, dx * 2 + dy, zs], "core")
+
+    def hops(self, r, dx, dy, j, act):
+        links, zs = self.links, self.links.spots[j]
+        z, same = links.z, j == ZN - 1
+        own = same and not dx and not dy
+        for d in onward(ROUTES[self.parts[r][4]], dx, dy, same):
+            if d != "z":
+                act(self.hop(r, dx, dy, zs, d, own))
+                continue
+            up = links.above if same else jnp.logical_and(z > zs, links.above)
+            down = links.below if same else jnp.logical_and(z < zs, links.below)
+            pl.when(up)(lambda: act(self.hop(r, dx, dy, zs, "up", own)))
+            pl.when(down)(lambda: act(self.hop(r, dx, dy, zs, "dn", own)))
+
+    def forward(self, event):
+        _, r, dx, dy, j = event
+        zs, own = self.links.spots[j], j == ZN - 1 and not dx and not dy
+        if not own:
+            self.links.copy(self.dst(r, dx, dy, zs), self.dst(r, dx, dy, zs), self.send.at[r, 0, 0, 0],
+                            self.recv.at[r, dx * 2 + dy, zs], "core").wait_recv()
+        self.hops(r, dx, dy, j, lambda copy: copy.start())
+        self.across(r, dx, dy, zs, own).start()
+        if own:
+            self.local(r).start()
+
+    def local(self, r):
+        return pltpu.make_async_copy(self.ins[self.parts[r][0]].at[self.window(r)],
+                                     self.dst(r, 0, 0, self.links.z), self.lsem.at[r])
+
+    def finish(self):
+        for _, r, dx, dy, j in self.events:
+            own = j == ZN - 1 and not dx and not dy
+            self.hops(r, dx, dy, j, lambda copy: copy.wait_send())
+            copy = self.across(r, dx, dy, self.links.spots[j], own)
+            copy.wait_send()
+            copy.wait_recv()
+            if own:
+                self.local(r).wait()
+
+
+def gather(parts, ins, rows):
+    n = len(ins)
+
+    def kernel(*refs):
+        job = Gather(parts, refs[:n], refs[n : n + len(rows)], *refs[n + len(rows) :])
+        job.links.greet()
+        for event in job.events:
+            job.forward(event)
+        job.finish()
+    anywhere = pl.BlockSpec(memory_space=pl.ANY)
+    return pl.pallas_call(
+        kernel,
+        out_shape=[jax.ShapeDtypeStruct((8 * ZN, count, W), jnp.bfloat16) for count in rows],
+        in_specs=[anywhere] * n,
+        out_specs=[anywhere] * len(rows),
+        scratch_shapes=Gather.scratch(parts),
+        compiler_params=pltpu.CompilerParams(collective_id=1, has_side_effects=True),
+    )(*ins)
+
+
+def layout(order):
+    base, count = {}, 0
+    for i, d in enumerate(order):
+        base[d] = count
+        free = 1
+        for e in order[:i]:
+            free *= ZN if e == "z" else 2
+        count += free * ((ZN + 1) if d == "z" else 1)
+    return base, count
+
+
+class Scatter:
+    def __init__(self, parts, ins, out, sib, stage, send, csend, crecv, lsem, *rest):
+        self.parts, self.ins, self.out, self.sib, self.stage = parts, ins, out, sib, stage
+        self.send, self.csend, self.crecv, self.lsem = send, csend, crecv, lsem
+        self.bufs, self.recv = rest[: len(parts)], rest[len(parts) :]
+        self.links = Links()
+        self.events = sorted(blocks(parts), key=lambda e: -e[0])
+        self.lay = [layout(ROUTES[part[3]]) for part in parts]
+        self.starts = [sum(part[2] for part in parts[:r]) for r in range(len(parts))]
+
+    @staticmethod
+    def scratch(parts):
+        n, total = len(parts), sum(part[2] for part in parts)
+        counts = [layout(ROUTES[part[3]])[1] for part in parts]
+        most = max(part[2] for part in parts)
+        return [pltpu.VMEM((4, ZN, total, W), jnp.bfloat16), pltpu.VMEM((STG, most, W), jnp.bfloat16), SEM((n, 4, ZN)),
+                SEM((n, 4, ZN)), SEM((n, 4, ZN)), SEM((STG,))] + [
+            pltpu.VMEM((count, part[2], W), jnp.bfloat16) for count, part in zip(counts, parts)
+        ] + [SEM((count,)) for count in counts]
+
+    def mine(self, r):
+        return pl.ds(self.starts[r], self.parts[r][2])
+
+    def source(self, r, dx, dy, zd, core):
+        which, start, rows, _ = self.parts[r]
+        return self.ins[which].at[self.links.slot(dx, dy, zd, core), pl.ds(start, rows)]
+
+    def child(self, r, d, dx, dy, zd):
+        order = ROUTES[self.parts[r][3]]
+        dim = d if d in "xy" else "z"
+        index = 0
+        for e in order[: order.index(dim)]:
+            index = index * ZN + zd if e == "z" else index * 2 + (dx if e == "x" else dy)
+        if dim == "z":
+            index = index * (ZN + 1) + (zd if d == "up" else zd + 1)
+        return self.lay[r][0][dim] + index
+
+    def across(self, event):
+        _, r, dx, dy, j = event
+        zd = self.links.spots[j]
+        return self.links.copy(self.source(r, dx, dy, zd, 1 - self.links.c), self.sib.at[dx * 2 + dy, zd, self.mine(r)],
+                               self.csend.at[r, dx * 2 + dy, zd], self.crecv.at[r, dx * 2 + dy, zd], "core")
+
+    def load(self, i):
+        _, r, dx, dy, j = self.events[i]
+        return pltpu.make_async_copy(self.source(r, dx, dy, self.links.spots[j], self.links.c),
+                                     self.stage.at[i % STG, pl.ds(0, self.parts[r][2])], self.lsem.at[i % STG])
+
+    def hop(self, r, dx, dy, zd, d):
+        came = {"x": "x", "y": "y", "up": "dn", "dn": "up"}[d]
+        at = self.child(r, came, 0 if d == "x" else dx, 0 if d == "y" else dy, zd)
+        return self.links.copy(self.sib.at[dx * 2 + dy, zd, self.mine(r)], self.bufs[r].at[at],
+                               self.send.at[r, dx * 2 + dy, zd], self.recv[r].at[at], d)
+
+    def add(self, i, dirs):
+        _, r, dx, dy, j = self.events[i]
+        zd = self.links.spots[j]
+        final = j == ZN - 1 and not dx and not dy
+        at = [self.child(r, d, dx, dy, zd) for d in dirs]
+        for k in at:
+            self.links.copy(self.bufs[r].at[k], self.bufs[r].at[k], self.send.at[r, 0, 0], self.recv[r].at[k], "core").wait_recv()
+
+        def body(q, _):
+            low = pl.ds(pl.multiple_of(q * 16, 16), 16)
+            here = pl.ds(pl.multiple_of(self.starts[r] + q * 16, 16), 16)
+            total = self.stage[i % STG, low].astype(jnp.float32) + self.sib[dx * 2 + dy, zd, here].astype(jnp.float32)
+            for k in at:
+                total = total + self.bufs[r][k, low].astype(jnp.float32)
+            if final:
+                self.out[here] = total
+            else:
+                self.sib[dx * 2 + dy, zd, here] = total.astype(jnp.bfloat16)
+            return 0
+        lax.fori_loop(0, self.parts[r][2] // 16, body, 0)
+
+    def begin(self):
+        for event in self.events:
+            self.across(event).start()
+        for i in range(STG - 1):
+            self.load(i).start()
+
+    def step(self, i):
+        links = self.links
+        _, r, dx, dy, j = self.events[i]
+        zd, z, same = links.spots[j], links.z, j == ZN - 1
+        order = ROUTES[self.parts[r][3]]
+        if i + STG - 1 < len(self.events):
+            self.load(i + STG - 1).start()
+        self.load(i).wait()
+        self.across(self.events[i]).wait_recv()
+        kids = onward(order, dx, dy, same)
+        fixed = [d for d in kids if d != "z"]
+        if "z" not in kids:
+            self.add(i, fixed)
+        elif same:
+            pl.when(z == 0)(lambda: self.add(i, fixed + ["up"]))
+            pl.when(z == ZN - 1)(lambda: self.add(i, fixed + ["dn"]))
+            pl.when(jnp.logical_and(links.below, links.above))(lambda: self.add(i, fixed + ["up", "dn"]))
+        else:
+            pl.when(jnp.logical_and(z > zd, links.above))(lambda: self.add(i, fixed + ["up"]))
+            pl.when(jnp.logical_and(z < zd, links.below))(lambda: self.add(i, fixed + ["dn"]))
+            pl.when(jnp.logical_or(z == 0, z == ZN - 1))(lambda: self.add(i, fixed))
+        if not (same and not dx and not dy):
+            d = arrival(order, dx, dy, same)
+            if d == "z":
+                pl.when(zd > z)(lambda: self.hop(r, dx, dy, zd, "up").start())
+                pl.when(zd < z)(lambda: self.hop(r, dx, dy, zd, "dn").start())
+            else:
+                self.hop(r, dx, dy, zd, d).start()
+
+    def finish(self):
+        for event in self.events:
+            _, r, dx, dy, j = event
+            self.across(event).wait_send()
+            if not (j == ZN - 1 and not dx and not dy):
+                self.hop(r, dx, dy, self.links.spots[j], "x").wait_send()
+
+
+def scatter(parts, ins):
+    n, total = len(ins), sum(part[2] for part in parts)
+
+    def kernel(*refs):
+        job = Scatter(parts, refs[:n], *refs[n:])
+        job.links.greet()
+        job.begin()
+        for i in range(len(job.events)):
+            job.step(i)
+        job.finish()
+    return pl.pallas_call(
+        kernel,
+        out_shape=jax.ShapeDtypeStruct((total, W), jnp.float32),
+        in_specs=[pl.BlockSpec(memory_space=pl.ANY)] * n,
+        out_specs=pl.BlockSpec(memory_space=pltpu.VMEM),
+        scratch_shapes=Scatter.scratch(parts),
+        compiler_params=pltpu.CompilerParams(collective_id=2, has_side_effects=True, vmem_limit_bytes=62 << 20),
+    )(*ins)
+
+
+RATE_AT, ENTRY_AT, OUT_AT, GATE_AT, INPUT_AT, REC_ROWS = 0, 144, 288, 384, 480, 576
+FFN_GATE_AT, FFN_UP_AT, FFN_DOWN_AT, SMALL_AT, SMALL_ROWS = 576, 768, 960, 1152, 16
+GATHER_PARTS = ((0, 0, 0, 288, 0), (0, 0, 288, 288, 1), (0, 0, 576, 288, 2), (0, 0, 864, 304, 3))
+SCATTER_PARTS = ((0, 0, 288, 0), (0, 288, 288, 1), (1, 0, 288, 2), (1, 288, 288, 3), (2, 0, 16, 0))
+
+
+def pack_blocks(item):
+    rows, cols = item.shape
+    return item.reshape(rows, cols // W, W).transpose(1, 0, 2).reshape(rows * cols // W, W)
+
+
+def unpack_blocks(item, rows, cols):
+    return item.reshape(cols // W, rows, W).transpose(1, 0, 2).reshape(rows, cols)
+
+
+def pad_rows(item, before, count):
+    batch, rows, cols = item.shape
+    item = jnp.pad(item, ((0, 0), (before, count - rows - before), (0, 0)))
+    return item.reshape(batch * count, cols)
+
+
+def per_device_packed(tokens, cotangent, lengths, *shards):
+    (gate_proj, input_proj, rate_proj, entry_proj, out_proj, ffn_gate, ffn_up, ffn_down) = shards[:8]
+    small = shards[8:]
+    batch, width, depth = tokens.shape
+    r, f = gate_proj.shape[1], ffn_gate.shape[1]
+    n_seq = lax.axis_size("seq")
+    me = lax.axis_index("seq")
+    rim = pad_rows(from_behind(tokens[:, width - 3 :], "seq", 1), 5, 8)
+    flat = jnp.concatenate([item.reshape(-1) for item in small])
+    flat = jnp.pad(flat, (0, SMALL_ROWS * W - flat.shape[0])).reshape(SMALL_ROWS, W)
+    order = (rate_proj, entry_proj, out_proj, gate_proj, input_proj, ffn_gate, ffn_up, ffn_down)
+    packed = gather(GATHER_PARTS, [jnp.concatenate([pack_blocks(item) for item in order] + [flat], axis=0)], [SMALL_AT + SMALL_ROWS])[0]
+    flats = packed[:, SMALL_AT].astype(jnp.float32)
+    lo, vectors = 0, []
+    for item in small:
+        part = flats[:, lo : lo + item.size]
+        lo += item.size
+        if item.ndim == 2:
+            part = part.reshape(-1, *item.shape).transpose(1, 0, 2).reshape(item.shape[0], -1)
+        else:
+            part = part.reshape(1, -1)
+        vectors.append(part)
+    norm_gain, ffn_gain, taps, conv_bias, rate_bias, entry_bias, logit = vectors
+    vec = jnp.concatenate([taps, conv_bias, rate_bias, entry_bias, -lru_scale * jax.nn.softplus(-logit),
+                           jax.nn.sigmoid(-logit), jnp.zeros((7, r), jnp.float32)], axis=0)
+    norm_gain = jnp.broadcast_to(norm_gain, (8, depth))
+    ffn_gain = jnp.broadcast_to(ffn_gain, (8, depth))
+    info = jnp.concatenate([jnp.clip(lengths - me * width, 0, width), me[None]]).astype(jnp.int32)
+    tokens2 = tokens.reshape(batch * width, depth)
+    cot2 = cotangent.reshape(batch * width, depth)
+
+    gate_pre, inner, mixed, normed = branch(tokens2, rim, norm_gain, packed, vec, batch)
+    rate, entry, decay, drive, pseg, hseg, ends = gates(info, mixed, packed, vec, batch)
+    pall = exchange(ends, n_seq, 3)
+    states, sstart, gated, first, normed_two = states_and_first(
+        info, decay, drive, gate_pre, pseg, hseg, pall, tokens2, packed, ffn_gain, batch)
+    block_out, d_first, d_low, g_ffn_gain, grad_ffn = feed_forward(info, first, normed_two, cot2, ffn_gain, packed, f, batch)
+    d_states, d_gate, gseg, gtot, grad_rec = unproject(d_low, packed, gated, gate_pre, states, decay, pseg, batch)
+    gall = exchange(gtot, n_seq, 4)
+    d_mixed, sums, grad_rec = recur_back(
+        info, mixed, decay, d_states, states, rate, entry, pseg, gseg, sstart, pall, gall, vec, packed, grad_rec, batch)
+    rim_back = from_behind(d_mixed.reshape(batch, width, r)[:, :3].astype(jnp.bfloat16), "seq", -1)
+    rim_back = pad_rows(rim_back.astype(jnp.float32), 0, 8)
+    csums, token_grad, g_norm_gain, grad_rec = entry_back(
+        d_mixed, rim_back, inner, d_gate, normed, packed, vec, tokens2, d_first, norm_gain, grad_rec, batch)
+
+    n = packed.shape[0]
+    lines = [jnp.sum(g_norm_gain, axis=0).reshape(n, -1), jnp.sum(g_ffn_gain, axis=0).reshape(n, -1),
+             csums[:4].reshape(4, n, -1).transpose(1, 0, 2).reshape(n, -1), csums[4].reshape(n, -1),
+             sums[1].reshape(n, -1), sums[2].reshape(n, -1), sums[0].reshape(n, -1)]
+    lines = jnp.concatenate(lines, axis=1).astype(jnp.bfloat16)
+    lines = jnp.pad(lines, ((0, 0), (0, SMALL_ROWS * W - lines.shape[1]))).reshape(n, SMALL_ROWS, W)
+    total = scatter(SCATTER_PARTS, [grad_ffn, grad_rec, lines])
+    fr = REC_ROWS
+    at = {"rate": fr + RATE_AT, "entry": fr + ENTRY_AT, "out": fr + OUT_AT, "gate": fr + GATE_AT, "input": fr + INPUT_AT}
+    result = [(at["gate"], gate_proj), (at["input"], input_proj), (at["rate"], rate_proj), (at["entry"], entry_proj),
+              (at["out"], out_proj), (0, ffn_gate), (FFN_UP_AT - FFN_GATE_AT, ffn_up), (FFN_DOWN_AT - FFN_GATE_AT, ffn_down)]
+    result = [unpack_blocks(total[lo : lo + item.size // W], *item.shape) for lo, item in result]
+    flat = total[SMALL_AT]
+    lo = 0
+    for item in small:
+        result.append(flat[lo : lo + item.size].reshape(item.shape))
+        lo += item.size
+    return (block_out.reshape(tokens.shape), token_grad.reshape(tokens.shape), *result)
+
+
 def solution(mesh):
+    packs = mesh.shape["seq"] == 8 and mesh.shape["batch"] == ZN
     placed = (
         P("batch", "seq", None),
         P("batch", "seq", None),
@@ -513,7 +1662,7 @@
         P(("seq", "batch")),
     )
     return jax.shard_map(
-        per_device,
+        per_device_packed if packs else per_device,
         mesh=mesh,
         in_specs=placed,
         out_specs=(

time: 2440 us -> 561 us (0.23); the launches traced: 2410 us -> 552 us
  local copies, waits for them, and re-layouts: 1240 us -> 32.3 us
  other arithmetic: 566 us -> 6.41 us
  Pallas kernels: 0 us -> 507 us
  matrix products: 183 us -> 0 us
  blocking collectives: 172 us -> 0 us
  waiting for transfers between devices: 150 us -> 1.36 us
  starting transfers between devices: 75.5 us -> 3.03 us
    pallas_call x0 -> x11, Pallas kernels: none -> 507 us  [the longest x1 165 us: scatter(): pl.pallas_call(kernel, out_shape=jax.ShapeDtypeStruct((total, W), jnp.flo...]
    slice x225 -> x13, local copies, waits for them, and re-layouts: 429 us -> 8.16 us  [the longest x3 3.56 us: per_device_packed(): total[lo:lo + item.size // W]]
    convert_element_type x15 -> x0, local copies, waits for them, and re-layouts: 388 us -> none  [the longest x1 57.7 us: reduce_grads(): shaped[5].astype(jnp.bfloat16)]
    unnamed x17 -> x0, other arithmetic: 252 us -> none
    unnamed x540 -> x54, local copies, waits for them, and re-layouts: 225 us -> 9.99 us
    dot_general x48 -> x0, matrix products: 183 us -> none  [the longest x16 72.1 us: project_back(): jnp.einsum('bte,de->btd', left, right, preferred_element_type=jnp.float32)]
    pad x112 -> x2, local copies, waits for them, and re-layouts: 147 us -> 0.05 us  [the longest x1 0.04 us: per_device_packed(): jnp.pad(lines, ((0, 0), (0, SMALL_ROWS * W - lines.shape[1])))]
    all_gather x9 -> x0, blocking collectives: 132 us -> none  [the longest x1 62.4 us: fetch(): lax.all_gather(conv_taps, ('seq', 'batch'), axis=1, tiled=True)]
  transfers between devices with their start and end apart: 42 -> 2, of which waited for: 7 -> 1; matrix products, arithmetic and copies ran while one was open for 63% -> 2% of each run, Pallas kernels for 0% -> 26%
where the time goes in v1:
time: 561 us; the launch traced here: 552 us
  Pallas kernels  507 us (90%)
  local copies, waits for them, and re-layouts  32.3 us (6%)
  other arithmetic  6.41 us (1%)
    pallas_call x1, Pallas kernels, scatter(): pl.pallas_call(kernel, out_shape=jax.ShapeDtypeStruct((total, W), jnp.flo...  165 us
    pallas_call x1, Pallas kernels, gather(): pl.pallas_call(kernel, out_shape=[jax.ShapeDtypeStruct((8 * ZN, count, W)...  146 us
    pallas_call x1, Pallas kernels, feed_forward(): pl.pallas_call(functools.partial(ffn_kernel, batch, width), grid=(nd + nw...  58.8 us
    pallas_call x1, Pallas kernels, recur_back(): pl.pallas_call(functools.partial(recur_kernel, batch, width, n_seq), grid...  32.8 us
    pallas_call x1, Pallas kernels, entry_back(): pl.pallas_call(functools.partial(entry_kernel, batch, width), grid=(r //...  21.1 us
    pallas_call x1, Pallas kernels, gates(): pl.pallas_call(functools.partial(gates_kernel, batch, width), grid=(r //...  19.3 us
    pallas_call x2, Pallas kernels, exchange(): pl.pallas_call(functools.partial(exchange_kernel, n), out_shape=jax.Shape...  17.9 us
    pallas_call x1, Pallas kernels, states_and_first(): pl.pallas_call(functools.partial(states_kernel, batch, width, everyone.sh...  17.6 us
  transfers between devices with their start and end apart: 2, of which 1 were waited for; matrix products, arithmetic and copies ran while one was open for 2% of the time, Pallas kernels for 26%

profile of v1, /device:TPU:16, one launch (start us, length us, event | category | flops | bytes accessed | tf_op | source)
XLA Modules:
  0.0 551.6 jit_solution(746255645748081672)
XLA Ops:
  0.7 0.8 slice.123
  1.5 1.7 collective-permute-start
  4.0 4.1 concatenate.17
  8.2 0.9 copy.92
  9.1 1.0 reshape.294
  10.1 1.0 reshape.296
  11.1 1.0 reshape.288
  13.2 1.0 copy-done.12
  14.2 146.0 %shard_map.305.wg_ref.wi_ref.wr_ref.we_ref.wo_ref.wu_ref.wd_ref = bf16[32,1168,512]{2,1,0:T(8,128)(2,1)} custom-call(bf16[1168,512]{1,0:T(8,128)(2,1)} %copy-done.12), custom_call_target="tpu_custom_call" | custom-call | tf_op jit(solution)/shard_map/pallas_call | solution.py:1396
  160.3 1.1 slice_convert_fusion
  162.7 11.1 %shard_map.306 = (f32[12,512,128]{2,1,0:T(8,128)}, f32[528,1536]{1,0:T(8,128)}, bf16[512,1536]{1,0:T(8,128)(2,1)S(1)}, bf16[512,1024]{1,0:T(8,128)(2,1)S(1)}) custom-call(bf16[512,1024]{1,0:T(8,128)(2,1)S(1)} %bitcast.97, bf16[16,1024]{1,0:T(8,128)(2,1)S(1)} %pad_bitcast_fusion.rim_ref, f32[8,1024]{1,0:T(8,128)S(1)} %broadcast_in_dim.22.gain_ref, ...), custom_call_target="tpu_custom_call" | custom-call | tf_op jit(solution)/shard_map/pallas_call | solution.py:635
  173.9 19.3 %shard_map.307 = (f32[12,512,128]{2,1,0:T(8,128)}, f32[12,512,128]{2,1,0:T(8,128)}, f32[12,512,128]{2,1,0:T(8,128)}, f32[12,512,128]{2,1,0:T(8,128)}, f32[16,153...) custom-call(s32[3]{0:T(128)S(1)} %pad_add_fusion.info_ref, ...), custom_call_target="tpu_custom_call" | custom-call | tf_op jit(solution)/shard_map/pallas_call | solution.py:702
  193.8 9.4 %shard_map.308.all_ref.pall_ref = f32[8,8,1536]{2,1,0:T(8,128)} custom-call(f32[8,1536]{1,0:T(8,128)} %copy-done.10), custom_call_target="tpu_custom_call" | custom-call | tf_op jit(solution)/shard_map/pallas_call | solution.py:737
  203.2 1.0 copy-done.2
  204.2 17.6 %shard_map.309 = (f32[12,512,128]{2,1,0:T(8,128)}, f32[16,1536]{1,0:T(8,128)S(1)}, bf16[512,1536]{1,0:T(8,128)(2,1)}, f32[512,1024]{1,0:T(8,128)}, bf16[512,1024]{1,0:T(8,128)(2,1)S(1)}) custom-call(s32[3]{0:T(128)S(1)} %pad_add_fusion.info_ref, f32[12,512,128]{2,1,0:T(8,128)} %get-tuple-element.51.decay_ref, f32[12,512,128]{2,1,0:T(8,128)} %get-tuple-element.52.drive_ref, ...), custom_call_target="tpu_custom_call" | custom-call | tf_op jit(solution)/shard_map/pallas_call | solution.py:805
  221.8 0.9 copy-done.5
  223.4 58.8 %shard_map.310 = (f32[512,1024]{1,0:T(8,128)}, f32[512,1024]{1,0:T(8,128)}, bf16[512,1024]{1,0:T(8,128)(2,1)}, f32[8,1024]{1,0:T(8,128)}, bf16[32,576,512]{2,1,0:T(8,128)(2,1)}) custom-call(s32[3]{0:T(128)} %copy-done.11, f32[512,1024]{1,0:T(8,128)} %get-tuple-element.57.first_ref, bf16[512,1024]{1,0:T(8,128)(2,1)} %copy-done.5, ...), custom_call_target="tpu_custom_call" | custom-call | tf_op jit(solution)/shard_map/pallas_call | solution.py:951
  282.2 17.3 %shard_map.311 = (f32[12,512,128]{2,1,0:T(8,128)}, bf16[512,1536]{1,0:T(8,128)(2,1)}, f32[16,1536]{1,0:T(8,128)}, f32[8,1536]{1,0:T(8,128)}, bf16[32,576,512]{2,1,0:T(8,128)(2,1)}) custom-call(bf16[512,1024]{1,0:T(8,128)(2,1)} %get-tuple-element.60.dlow_ref, bf16[32,1168,512]{2,1,0:T(8,128)(2,1)} %shard_map.305.wg_ref.wi_ref.wr_ref.we_ref.wo_ref.wu_ref.wd_ref, ...), custom_call_target="tpu_custom_call" | custom-call | tf_op jit(solution)/shard_map/pallas_call | solution.py:1022
  299.6 8.5 %shard_map.312.gall_ref = f32[8,8,1536]{2,1,0:T(8,128)} custom-call(f32[8,1536]{1,0:T(8,128)} %get-tuple-element.68.x_ref), custom_call_target="tpu_custom_call" | custom-call | tf_op jit(solution)/shard_map/pallas_call | solution.py:737
  308.1 32.8 %shard_map.313 = (f32[512,1536]{1,0:T(8,128)}, f32[8,1536]{1,0:T(8,128)}, bf16[32,576,512]{2,1,0:T(8,128)(2,1)}) custom-call(s32[3]{0:T(128)} %copy-done.11, bf16[512,1536]{1,0:T(8,128)(2,1)} %copy-done.1, f32[12,512,128]{2,1,0:T(8,128)} %get-tuple-element.51.decay_ref, ...), custom_call_target="tpu_custom_call", output_to_operand_aliasing={{2}: (15, {})} | custom-call | tf_op jit(solution)/shard_map/pallas_call | solution.py:1136
  341.8 2.1 convert.37
  343.9 1.3 collective-permute-start.1
  345.6 1.4 collective-permute-done.1
  347.6 21.1 %shard_map.314 = (f32[8,1536]{1,0:T(8,128)}, f32[512,1024]{1,0:T(8,128)}, f32[8,1024]{1,0:T(8,128)}, bf16[32,576,512]{2,1,0:T(8,128)(2,1)}) custom-call(f32[512,1536]{1,0:T(8,128)} %get-tuple-element.70.dmixed_ref, f32[16,1536]{1,0:T(8,128)} %bitcast_convert_fusion.rim_ref, ...), custom_call_target="tpu_custom_call", output_to_operand_aliasing={{3}: (11, {})} | custom-call | tf_op jit(solution)/shard_map/pallas_call | solution.py:1216
  370.9 1.0 copy.78
  371.9 164.7 %shard_map.315 = f32[1168,512]{1,0:T(8,128)} custom-call(bf16[32,576,512]{2,1,0:T(8,128)(2,1)} %get-tuple-element.77.refs_0_, bf16[32,576,512]{2,1,0:T(8,128)(2,1)} %get-tuple-element.78.refs_1_, bf16[32,16,512]{2,1,0:T(8,128)(2,1)} %bitcast.99), custom_call_target="tpu_custom_call" | custom-call | tf_op jit(solution)/shard_map/pallas_call | solution.py:1545
  537.4 1.3 slice_bitcast_fusion.4
  538.7 1.4 slice_bitcast_fusion
  540.1 1.2 fusion.2
  541.2 1.1 fusion.3
  542.3 1.3 fusion.1
  548.5 0.8 copy.81
  (113 shorter events, 15.8 us)
Async XLA Ops:
  0.7 11.5 %copy-start.16 = (bf16[48,1536]{1,0:T(8,128)(2,1)S(1)}, bf16[48,1536]{1,0:T(8,128)(2,1)}, u32[]{:S(2)}) copy-start(bf16[48,1536]{1,0:T(8,128)(2,1)} %param.24) | copy-start | bytes 442372
  0.7 11.7 %copy-start.15 = (bf16[96,1024]{1,0:T(8,128)(2,1)S(1)}, bf16[96,1024]{1,0:T(8,128)(2,1)}, u32[]{:S(2)}) copy-start(bf16[96,1024]{1,0:T(8,128)(2,1)} %param.28) | copy-start | bytes 589828
  0.7 11.7 %copy-start.13 = (bf16[32,3072]{1,0:T(8,128)(2,1)S(1)}, bf16[32,3072]{1,0:T(8,128)(2,1)}, u32[]{:S(2)}) copy-start(bf16[32,3072]{1,0:T(8,128)(2,1)} %param.26) | copy-start | bytes 589828
  1.5 161.2 %collective-permute-start = (bf16[2,3,1024]{2,1,0:T(4,128)(2,1)S(1)}, bf16[2,3,1024]{2,1,0:T(4,128)(2,1)S(1)}, u32[]{:S(2)}, u32[]{:S(2)}) collective-permute-start(bf16[2,3,1024]{2,1,0:T(4,128)(2,1)S(1)} %slice.123), channel_id=1, source_target_pairs={{0,4},{4,8},{8,12},{12,16},{16,20},{20,24},{24,28},{1,5},{5,9},{9,... | collective-permute-start | bytes 36872 | tf_op jit(solution)/shard_map/ppermute | solution.py:20
  10.1 2.6 copy-start.14
  13.2 1.0 copy-start.12
  14.2 147.4 %copy-start.18 = (s32[2]{0:T(128)S(1)}, s32[2]{0:T(128)}, u32[]{:S(2)}) copy-start(s32[2]{0:T(128)} %param.20) | copy-start | bytes 28
  160.3 2.5 copy-start
  161.8 41.5 %copy-start.11 = (s32[3]{0:T(128)}, s32[3]{0:T(128)S(1)}, u32[]{:S(2)}) copy-start(s32[3]{0:T(128)S(1)} %pad_add_fusion.info_ref) | copy-start | bytes 40
  162.7 11.2 %copy-start.3 = (f32[16,1536]{1,0:T(8,128)}, f32[16,1536]{1,0:T(8,128)S(1)}, u32[]{:S(2)}) copy-start(f32[16,1536]{1,0:T(8,128)S(1)} %concatenate.19.vec_ref) | copy-start | bytes 294916
  162.7 11.1 %copy-start.7 = (f32[8,1024]{1,0:T(8,128)}, f32[8,1024]{1,0:T(8,128)S(1)}, u32[]{:S(2)}) copy-start(f32[8,1024]{1,0:T(8,128)S(1)} %broadcast_in_dim.22.gain_ref) | copy-start | bytes 98308
  173.8 19.3 %copy-start.1 = (bf16[512,1536]{1,0:T(8,128)(2,1)}, bf16[512,1536]{1,0:T(8,128)(2,1)S(1)}, u32[]{:S(2)}) copy-start(bf16[512,1536]{1,0:T(8,128)(2,1)S(1)} %get-tuple-element.50.mixed_ref) | copy-start | bytes 4718596
  173.8 19.3 %copy-start.4 = (bf16[512,1024]{1,0:T(8,128)(2,1)}, bf16[512,1024]{1,0:T(8,128)(2,1)S(1)}, u32[]{:S(2)}) copy-start(bf16[512,1024]{1,0:T(8,128)(2,1)S(1)} %get-tuple-element.73.normed_ref) | copy-start | bytes 3145732
  193.2 0.6 copy-start.10
  193.8 28.0 %copy-start.6 = (f32[16,1536]{1,0:T(8,128)}, f32[16,1536]{1,0:T(8,128)S(1)}, u32[]{:S(2)}) copy-start(f32[16,1536]{1,0:T(8,128)S(1)} %get-tuple-element.54.pseg_ref) | copy-start | bytes 294916
  203.2 18.6 %copy-start.8 = (f32[8,1024]{1,0:T(8,128)}, f32[8,1024]{1,0:T(8,128)S(1)}, u32[]{:S(2)}) copy-start(f32[8,1024]{1,0:T(8,128)S(1)} %broadcast_in_dim.25.gain_ref) | copy-start | bytes 98308
  203.2 1.0 copy-start.2
  221.8 1.0 copy-start.5
  222.8 0.6 copy-start.9
  341.8 3.5 copy-start.17
  343.9 3.1 collective-permute-start.1

commit v2 on v1

--- a/solution.py
+++ b/solution.py
@@ -592,234 +592,6 @@
     return total
 
 
-def branch_kernel(batch, width, x_ref, rim_ref, gain_ref, wg_ref, wi_ref, vec_ref,
-                  gate_ref, inner_ref, mixed_ref, normed_ref, ext):
-    step = pl.program_id(0)
-    tokens, depth = x_ref.shape
-    gain = gain_ref[:1]
-
-    @pl.when(step == 0)
-    def _():
-        def norm(i, _):
-            at = rows_at(i * CHUNK)
-            value = x_ref[at].astype(F32)
-            normed = (value * inverse_norm(value, depth) * gain).astype(BF16)
-            ext[at] = normed
-            normed_ref[at] = normed
-            return 0
-        lax.fori_loop(0, tokens // CHUNK, norm, 0)
-        rim = rim_ref[...].astype(F32)
-        ext[pl.ds(tokens, rim.shape[0])] = (rim * inverse_norm(rim, depth) * gain).astype(BF16)
-
-    spread(gate_ref, dot(ext[:tokens], wg_ref[...].reshape(depth, W)))
-    inner = dot(ext[...], wi_ref[...].reshape(depth, W))
-    span = width + 8
-    for b in range(batch):
-        inner_ref[b * span : b * span + 8] = inner[tokens + 8 * b : tokens + 8 * b + 8]
-        inner_ref[b * span + 8 : (b + 1) * span] = inner[b * width : (b + 1) * width]
-    for b in range(batch):
-        conv = vec_ref[CONV_BIAS : CONV_BIAS + 1]
-        for lag in range(4):
-            conv = conv + vec_ref[lag : lag + 1] * inner_ref[b * span + 8 - lag : (b + 1) * span - lag]
-        mixed_ref[b * width : (b + 1) * width] = conv.astype(BF16)
-
-
-def branch(tokens2, rim, gain, packed, vec, batch):
-    tokens, depth = tokens2.shape
-    width = tokens // batch
-    full = lambda a: pl.BlockSpec(a.shape, lambda j: (0,) * a.ndim)
-    r = vec.shape[1]
-    col = lambda rows: pl.BlockSpec((rows, W), lambda j: (0, j))
-    n = packed.shape[0]
-    rows = depth // n
-    return pl.pallas_call(
-        functools.partial(branch_kernel, batch, width),
-        grid=(r // W,),
-        in_specs=[full(tokens2), full(rim), full(gain),
-                  pl.BlockSpec((n, rows, W), lambda j: (0, GATE_AT // rows + j, 0)),
-                  pl.BlockSpec((n, rows, W), lambda j: (0, INPUT_AT // rows + j, 0)),
-                  col(vec.shape[0])],
-        out_specs=[tiled(tokens, W, lambda j: j), col(tokens + 8 * batch), col(tokens), pl.BlockSpec((tokens, depth), lambda j: (0, 0))],
-        out_shape=[jax.ShapeDtypeStruct((r // LANES, tokens, LANES), F32), jax.ShapeDtypeStruct((tokens + 8 * batch, r), F32),
-                   jax.ShapeDtypeStruct((tokens, r), BF16), jax.ShapeDtypeStruct((tokens, depth), BF16)],
-        scratch_shapes=[pltpu.VMEM((tokens + 8 * batch, depth), BF16)],
-        compiler_params=pltpu.CompilerParams(vmem_limit_bytes=50 << 20),
-    )(tokens2, rim, gain, packed, packed, vec)
-
-
-def gates_kernel(batch, width, info_ref, mixed_ref, wr_ref, we_ref, vec_ref,
-                 rate_ref, entry_ref, decay_ref, drive_ref, pseg_ref, hseg_ref, tot_ref):
-    step = pl.program_id(0)
-    r = mixed_ref.shape[1]
-    spread(rate_ref, dot(mixed_ref[...], wr_ref[...].reshape(r, W)))
-    spread(entry_ref, dot(mixed_ref[...], we_ref[...].reshape(r, W)))
-    tiles = W // LANES
-
-    def gating(t, b, spot, at, cols, _):
-        rate = sigmoid(rate_ref[t, at] + vec_ref[RATE_BIAS : RATE_BIAS + 1, cols])
-        entry = sigmoid(entry_ref[t, at] + vec_ref[ENTRY_BIAS : ENTRY_BIAS + 1, cols])
-        log_decay = vec_ref[COEF : COEF + 1, cols] * rate
-        z = 2.0 * log_decay
-        root = jnp.sqrt(one_less_exp(z, jnp.exp(z)))
-        valid = in_row(spot, width, rate.shape) < info_ref[b]
-        rate_ref[t, at] = rate
-        entry_ref[t, at] = entry
-        decay_ref[t, at] = jnp.where(valid, jnp.exp(log_decay), 1.0)
-        mixed = mixed_ref[at, pl.ds(pl.multiple_of(step * W + t * LANES, LANES), LANES)].astype(F32)
-        drive_ref[t, at] = jnp.where(valid, root * entry * mixed, 0.0)
-        return 0
-
-    each_tile(batch, width, tiles, gating)
-    tot_ref[...] = jnp.zeros_like(tot_ref)
-    for t in range(tiles):
-        cols = lanes(t)
-        for b in range(batch):
-            prod = jnp.ones((SEGS, LANES), F32)
-            state = jnp.zeros((SEGS, LANES), F32)
-            for s in range(width // SEGS):
-                at = strided(b, width, s)
-                a = decay_ref[t, at]
-                state = a * state + drive_ref[t, at]
-                prod = prod * a
-            pseg_ref[b * SEGS : (b + 1) * SEGS, cols] = prod
-            hseg_ref[b * SEGS : (b + 1) * SEGS, cols] = state
-            whole, end = prod[:1], state[:1]
-            for i in range(1, SEGS):
-                whole = whole * prod[i : i + 1]
-                end = prod[i : i + 1] * end + state[i : i + 1]
-            tot_ref[b : b + 1, cols] = whole
-            tot_ref[batch + b : batch + b + 1, cols] = end
-
-
-def gates(info, mixed, packed, vec, batch):
-    tokens, r = mixed.shape
-    width = tokens // batch
-    n = packed.shape[0]
-    rows = r // n
-    col = lambda count: pl.BlockSpec((count, W), lambda j: (0, j))
-    big = jax.ShapeDtypeStruct((r // LANES, tokens, LANES), F32)
-    seg = jax.ShapeDtypeStruct((batch * SEGS, r), F32)
-    return pl.pallas_call(
-        functools.partial(gates_kernel, batch, width),
-        grid=(r // W,),
-        in_specs=[pl.BlockSpec(memory_space=pltpu.SMEM), pl.BlockSpec((tokens, r), lambda j: (0, 0)),
-                  pl.BlockSpec((n, rows, W), lambda j: (0, RATE_AT // rows + j, 0)),
-                  pl.BlockSpec((n, rows, W), lambda j: (0, ENTRY_AT // rows + j, 0)),
-                  col(vec.shape[0])],
-        out_specs=[tiled(tokens, W, lambda j: j)] * 4 + [col(batch * SEGS)] * 2 + [col(8)],
-        out_shape=[big] * 4 + [seg] * 2 + [jax.ShapeDtypeStruct((8, r), F32)],
-        compiler_params=pltpu.CompilerParams(vmem_limit_bytes=50 << 20),
-    )(info, mixed, packed, packed, vec)
-
-
-def exchange_kernel(n, x_ref, o_ref, send, recv, own):
-    me, z = lax.axis_index("seq"), lax.axis_index("batch")
-    bar = pltpu.get_barrier_semaphore()
-    for k in range(1, n):
-        pl.semaphore_signal(bar, inc=1, device_id=(lax.rem(me + k, n), z), device_id_type=MESH)
-    pl.semaphore_wait(bar, n - 1)
-    mine = pltpu.make_async_copy(x_ref, o_ref.at[me], own)
-    mine.start()
-    copies = []
-    for k in range(1, n):
-        copies.append(pltpu.make_async_remote_copy(
-            x_ref, o_ref.at[me], send.at[k], recv.at[k],
-            device_id=(lax.rem(me + k, n), z), device_id_type=MESH))
-    for copy in copies:
-        copy.start()
-    mine.wait()
-    for copy in copies:
-        copy.wait()
-
-
-def exchange(value, n, ident):
-    D = pltpu.SemaphoreType.DMA
-    return pl.pallas_call(
-        functools.partial(exchange_kernel, n),
-        out_shape=jax.ShapeDtypeStruct((n,) + value.shape, value.dtype),
-        in_specs=[pl.BlockSpec(memory_space=pltpu.VMEM)],
-        out_specs=pl.BlockSpec(memory_space=pltpu.VMEM),
-        scratch_shapes=[D((n,)), D((n,)), D],
-        compiler_params=pltpu.CompilerParams(collective_id=ident, has_side_effects=True),
-    )(value)
-
-
-def states_kernel(batch, width, n_seq, info_ref, decay_ref, drive_ref, gate_ref, pseg_ref, hseg_ref, all_ref,
-                  x_ref, wo_ref, gain_ref, states_ref, sstart_ref, gated_ref, first_ref, normed_ref):
-    step = pl.program_id(0)
-    tokens, depth = x_ref.shape
-    r = gated_ref.shape[1]
-    parts = r // W
-
-    @pl.when(step < parts)
-    def _():
-        me = info_ref[batch]
-        for b in range(batch):
-            start = jnp.zeros((1, W), F32)
-            for k in range(n_seq):
-                new = all_ref[k, b : b + 1] * start + all_ref[k, batch + b : batch + b + 1]
-                start = jnp.where(k < me, new, start)
-            for i in range(SEGS):
-                at = b * SEGS + i
-                sstart_ref[at : at + 1] = start
-                start = pseg_ref[at : at + 1] * start + hseg_ref[at : at + 1]
-            for t in range(W // LANES):
-                state = sstart_ref[b * SEGS : (b + 1) * SEGS, lanes(t)]
-                for s in range(width // SEGS):
-                    at = strided(b, width, s)
-                    state = decay_ref[t, at] * state + drive_ref[t, at]
-                    states_ref[t, at] = state
-        j = jnp.minimum(step, parts - 1)
-
-        def gating(t, b, spot, at, cols, _):
-            gate = gelu_both(gate_ref[t, at])[0]
-            gated_ref[at, pl.ds(pl.multiple_of(j * W + t * LANES, LANES), LANES)] = (states_ref[t, at] * gate).astype(BF16)
-            return 0
-        each_tile(batch, width, W // LANES, gating)
-
-    for half in range(depth // W):
-        @pl.when(step == parts + half)
-        def _():
-            cols = slice(half * W, (half + 1) * W)
-            first_ref[:, cols] = x_ref[:, cols].astype(F32) + dot(gated_ref[...], wo_ref[...].reshape(r, W))
-
-    @pl.when(step == pl.num_programs(0) - 1)
-    def _():
-        def norm(i, _):
-            at = rows_at(i * CHUNK)
-            value = first_ref[at]
-            normed_ref[at] = (value * inverse_norm(value, depth) * gain_ref[:1]).astype(BF16)
-            return 0
-        lax.fori_loop(0, tokens // CHUNK, norm, 0)
-
-
-def states_and_first(info, decay, drive, gate_pre, pseg, hseg, everyone, tokens2, packed, gain, batch):
-    tokens, depth = tokens2.shape
-    r = pseg.shape[1]
-    width = tokens // batch
-    n = packed.shape[0]
-    rows = r // n
-    parts = r // W
-    col = lambda count: pl.BlockSpec((count, W), lambda j: (0, jnp.minimum(j, parts - 1)))
-    full = lambda shape: pl.BlockSpec(shape, lambda j: (0,) * len(shape))
-    return pl.pallas_call(
-        functools.partial(states_kernel, batch, width, everyone.shape[0]),
-        grid=(parts + depth // W,),
-        in_specs=[pl.BlockSpec(memory_space=pltpu.SMEM)] + [tiled(tokens, W, lambda j: jnp.minimum(j, parts - 1))] * 3 + [
-                  col(batch * SEGS), col(batch * SEGS),
-                  pl.BlockSpec((everyone.shape[0], 8, W), lambda j: (0, 0, jnp.minimum(j, parts - 1))),
-                  full(tokens2.shape),
-                  pl.BlockSpec((n, rows, W), lambda j: (0, OUT_AT // rows + jnp.maximum(j - parts, 0), 0)),
-                  full(gain.shape)],
-        out_specs=[tiled(tokens, W, lambda j: jnp.minimum(j, parts - 1)), col(batch * SEGS), full((tokens, r)),
-                   full((tokens, depth)), full((tokens, depth))],
-        out_shape=[jax.ShapeDtypeStruct((r // LANES, tokens, LANES), F32), jax.ShapeDtypeStruct((batch * SEGS, r), F32),
-                   jax.ShapeDtypeStruct((tokens, r), BF16), jax.ShapeDtypeStruct((tokens, depth), F32),
-                   jax.ShapeDtypeStruct((tokens, depth), BF16)],
-        compiler_params=pltpu.CompilerParams(vmem_limit_bytes=50 << 20),
-    )(info, decay, drive, gate_pre, pseg, hseg, everyone, tokens2, packed, gain)
-
-
 def put(stage, sem, slot, dst, value, used):
     copy = pltpu.make_async_copy(stage.at[slot], dst, sem.at[slot])
     if used is True:
@@ -970,8 +742,10 @@
 
 
 def unproject_kernel(batch, width, dlow_ref, wo_ref, gated_ref, gate_ref, states_ref, decay_ref, pseg_ref,
-                     dstates_ref, dgate_ref, gseg_ref, gtot_ref, grad_ref, stage, sem):
+                     dstates_ref, dgate_ref, gseg_ref, all_ref, grad_ref, stage, sem, gtot_ref, *rest):
     step = pl.program_id(0)
+    swap = Exchange(all_ref.shape[0], gtot_ref, *rest)
+    pl.when(step == 0)(lambda: greet(None, swap))
     tokens, depth = dlow_ref.shape
     orows = wo_ref.shape[1] // 2
     group = wo_ref.shape[0]
@@ -990,7 +764,6 @@
         value = dot_outer(gated_ref[...], dlow_ref[:, half * W : (half + 1) * W]).astype(BF16)
         dst = grad_ref.at[pl.ds(step * group, group), pl.ds(OUT_AT + half * orows, orows)]
         put(stage, sem, half, dst, value.reshape(group, orows, W), step > 0)
-    gtot_ref[...] = jnp.zeros_like(gtot_ref)
     for t in range(wide // LANES):
         cols = lanes(t)
         for b in range(batch):
@@ -1002,15 +775,18 @@
             whole = grad[SEGS - 1 :]
             for i in reversed(range(SEGS - 1)):
                 whole = grad[i : i + 1] + pseg_ref[b * SEGS + i : b * SEGS + i + 1, cols] * whole
-            gtot_ref[b : b + 1, cols] = whole
+            gtot_ref[step * (wide // LANES) + t, b : b + 1] = whole
 
     @pl.when(step == pl.num_programs(0) - 1)
     def _():
         for half in range(2):
             pltpu.make_async_copy(stage.at[half], grad_ref.at[pl.ds(0, group), pl.ds(OUT_AT, orows)], sem.at[half]).wait()
-
-
-def unproject(dlow, packed, gated, gate_pre, states, decay, pseg, batch):
+        swap.begin()
+        swap.finish()
+        all_ref[...] = swap.land[...]
+
+
+def unproject(dlow, packed, gated, gate_pre, states, decay, pseg, batch, n_seq):
     tokens, r = gated.shape
     depth = dlow.shape[1]
     width = tokens // batch
@@ -1025,13 +801,14 @@
         in_specs=[pl.BlockSpec((tokens, depth), lambda j: (0, 0)),
                   pl.BlockSpec((group, 2 * orows, W), lambda j: (j, OUT_AT // (2 * orows), 0)),
                   col(tokens)] + [tiled(tokens, wide, lambda j: j)] * 3 + [col(batch * SEGS)],
-        out_specs=[tiled(tokens, wide, lambda j: j), col(tokens), col(batch * SEGS), col(8), pl.BlockSpec(memory_space=pl.ANY)],
+        out_specs=[tiled(tokens, wide, lambda j: j), col(tokens), col(batch * SEGS),
+                   pl.BlockSpec((n_seq, r // LANES, batch, LANES), lambda j: (0, 0, 0, 0)), pl.BlockSpec(memory_space=pl.ANY)],
         out_shape=[jax.ShapeDtypeStruct((r // LANES, tokens, LANES), F32), jax.ShapeDtypeStruct((tokens, r), BF16),
-                   jax.ShapeDtypeStruct((batch * SEGS, r), F32), jax.ShapeDtypeStruct((8, r), F32),
+                   jax.ShapeDtypeStruct((batch * SEGS, r), F32), jax.ShapeDtypeStruct((n_seq, r // LANES, batch, LANES), F32),
                    jax.ShapeDtypeStruct((n, REC_ROWS, W), BF16)],
         scratch_shapes=[pltpu.VMEM((2, group, orows, W), BF16),
-                        pltpu.SemaphoreType.DMA((2,))],
-        compiler_params=pltpu.CompilerParams(vmem_limit_bytes=60 << 20),
+                        pltpu.SemaphoreType.DMA((2,))] + Exchange.scratch(n_seq, (r // LANES, batch, LANES)),
+        compiler_params=pltpu.CompilerParams(collective_id=4, has_side_effects=True, vmem_limit_bytes=60 << 20),
     )(dlow, packed, gated, gate_pre, states, decay, pseg)
 
 
@@ -1050,16 +827,17 @@
     def _():
         me = info_ref[batch]
         for b in range(batch):
-            grad = jnp.zeros((1, W), F32)
-            for k in reversed(range(n_seq)):
-                new = pall_ref[k, b : b + 1] * grad + gall_ref[k, b : b + 1]
-                grad = jnp.where(k > me, new, grad)
-            for i in reversed(range(SEGS)):
-                at = b * SEGS + i
-                gstart[i : i + 1] = grad
-                grad = pseg_ref[at : at + 1] * grad + gseg_ref[at : at + 1]
             for t in range(W // LANES):
-                grad = gstart[:, lanes(t)]
+                cols = lanes(t)
+                grad = jnp.zeros((1, LANES), F32)
+                for k in reversed(range(n_seq)):
+                    new = pall_ref[k, t, b : b + 1] * grad + gall_ref[k, t, b : b + 1]
+                    grad = jnp.where(k > me, new, grad)
+                for i in reversed(range(SEGS)):
+                    at = b * SEGS + i
+                    gstart[i : i + 1, cols] = grad
+                    grad = pseg_ref[at : at + 1, cols] * grad + gseg_ref[at : at + 1, cols]
+                grad = gstart[:, cols]
                 for s in reversed(range(width // SEGS)):
                     at = strided(b, width, s)
                     total = dstates_ref[t, at] + grad
@@ -1130,14 +908,14 @@
     wide = group * rows
     n_seq = pall.shape[0]
     col = lambda count: pl.BlockSpec((count, W), lambda j: (0, jnp.minimum(j, parts - 1)))
-    over = pl.BlockSpec((n_seq, 8, W), lambda j: (0, 0, jnp.minimum(j, parts - 1)))
+    over = lambda a: pl.BlockSpec((n_seq, W // LANES) + a.shape[2:], lambda j: (0, jnp.minimum(j, parts - 1), 0, 0))
     later = lambda j: jnp.maximum(j - parts, 0)
     vm = pltpu.VMEM
     return pl.pallas_call(
         functools.partial(recur_kernel, batch, width, n_seq),
         grid=(parts + n // group,),
         in_specs=[pl.BlockSpec(memory_space=pltpu.SMEM), pl.BlockSpec((tokens, r), lambda j: (0, 0))]
-        + [tiled(tokens, W, lambda j: jnp.minimum(j, parts - 1))] * 5 + [col(batch * SEGS)] * 3 + [over, over, col(vec.shape[0]),
+        + [tiled(tokens, W, lambda j: jnp.minimum(j, parts - 1))] * 5 + [col(batch * SEGS)] * 3 + [over(pall), over(gall), col(vec.shape[0]),
             pl.BlockSpec((group, parts * rows, W), lambda j: (later(j), RATE_AT // (parts * rows), 0)),
             pl.BlockSpec((group, parts * rows, W), lambda j: (later(j), ENTRY_AT // (parts * rows), 0)),
             pl.BlockSpec(memory_space=pl.ANY)],
@@ -1274,22 +1052,64 @@
         self.spots = [far(z, j) for j in range(ZN)]
         self.above, self.below = z < ZN - 1, z > 0
 
-    def greet(self):
-        bar = pltpu.get_barrier_semaphore()
-
-        def signal(d):
-            pl.semaphore_signal(bar, inc=1, device_id=self.beside[d], device_id_type=MESH)
-        for d in ("x", "y", "core"):
-            signal(d)
-        pl.when(self.above)(lambda: signal("up"))
-        pl.when(self.below)(lambda: signal("dn"))
-        pl.semaphore_wait(bar, 3 + self.above.astype(jnp.int32) + self.below.astype(jnp.int32))
-
     def slot(self, dx, dy, z, core):
         return seq_of(flip(self.y, dy), flip(self.x, dx), core) * ZN + z
 
     def copy(self, src, dst, send, recv, d):
         return pltpu.make_async_remote_copy(src, dst, send, recv, device_id=self.beside[d], device_id_type=MESH)
+
+
+def greet(links, swap):
+    bar = pltpu.get_barrier_semaphore()
+    count = 0
+    if swap is not None:
+        count = swap.n - 1
+        for k in range(1, swap.n):
+            pl.semaphore_signal(bar, inc=1, device_id=swap.peer(k), device_id_type=MESH)
+    if links is not None:
+        def signal(d):
+            pl.semaphore_signal(bar, inc=1, device_id=links.beside[d], device_id_type=MESH)
+        if swap is None:
+            count = 3
+            for d in ("x", "y", "core"):
+                signal(d)
+        pl.when(links.above)(lambda: signal("up"))
+        pl.when(links.below)(lambda: signal("dn"))
+        count = count + links.above.astype(jnp.int32) + links.below.astype(jnp.int32)
+    pl.semaphore_wait(bar, count)
+
+
+class Exchange:
+    def __init__(self, n, rows, land, send, recv, own):
+        self.n, self.rows, self.land, self.send, self.recv, self.own = n, rows, land, send, recv, own
+        self.me, self.z = lax.axis_index("seq"), lax.axis_index("batch")
+
+    @staticmethod
+    def scratch(n, shape):
+        return [pltpu.VMEM(shape, F32), pltpu.VMEM((n,) + shape, F32), SEM((n,)), SEM((n,)), SEM]
+
+    def peer(self, k):
+        return (lax.rem(self.me + k, self.n), self.z)
+
+    def copies(self):
+        return [
+            pltpu.make_async_remote_copy(self.rows, self.land.at[self.me], self.send.at[k], self.recv.at[k],
+                                         device_id=self.peer(k), device_id_type=MESH)
+            for k in range(1, self.n)
+        ]
+
+    def mine(self):
+        return pltpu.make_async_copy(self.rows, self.land.at[self.me], self.own)
+
+    def begin(self):
+        self.mine().start()
+        for copy in self.copies():
+            copy.start()
+
+    def finish(self):
+        self.mine().wait()
+        for copy in self.copies():
+            copy.wait()
 
 
 def onward(order, dx, dy, same):
@@ -1388,7 +1208,7 @@
 
     def kernel(*refs):
         job = Gather(parts, refs[:n], refs[n : n + len(rows)], *refs[n + len(rows) :])
-        job.links.greet()
+        greet(job.links, None)
         for event in job.events:
             job.forward(event)
         job.finish()
@@ -1537,7 +1357,7 @@
 
     def kernel(*refs):
         job = Scatter(parts, refs[:n], *refs[n:])
-        job.links.greet()
+        greet(job.links, None)
         job.begin()
         for i in range(len(job.events)):
             job.step(i)
@@ -1552,9 +1372,255 @@
     )(*ins)
 
 
+class Sends:
+    def __init__(self, sems):
+        self.sems, self.used = sems, []
+
+    def add(self, src, dst):
+        copy = pltpu.make_async_copy(src, dst, self.sems.at[len(self.used)])
+        self.used.append(copy)
+        return copy
+
+    def finish(self):
+        for copy in self.used:
+            copy.wait()
+
+
+def spaced(events, slots):
+    bounds = [len(events) * i // slots for i in range(slots + 1)]
+    return [events[bounds[i] : bounds[i + 1]] for i in range(slots)]
+
+
+FORWARD_OUTS = 13
+
+
+def forward_kernel(batch, width, n_seq, info_ref, x_ref, rim_ref, gain_ref, gain2_ref, vec_ref,
+                   wg_ref, wi_ref, wr_ref, we_ref, wo_ref, shard_ref, *refs):
+    outs, refs = refs[:FORWARD_OUTS], refs[FORWARD_OUTS:]
+    (gate_o, inner_o, mixed_o, normed_o, rate_o, entry_o, decay_o, states_o, pseg_o, sstart_o, all_o,
+     gated_o, first_o) = outs
+    normed2_o, weights_o = refs[:2]
+    (ext, gate, inner, mixed, rate, entry, decay, drive, states, pseg, hseg, sstart, gated, first, normed2,
+     sems) = refs[2:18]
+    swap = Exchange(n_seq, *refs[18:23])
+    job = Gather(FFN_GATHER, [shard_ref], [weights_o], *refs[23:])
+    step = pl.program_id(0)
+    tokens, depth = x_ref.shape
+    r = mixed.shape[1]
+    parts, tiles, halves = r // W, W // LANES, depth // W
+    steps = 3 * parts + halves
+    span = width + 8
+    plan = spaced(job.events[len(FFN_GATHER) :], 2 * steps)
+
+    def pump(half, low, high):
+        for s in range(low, high):
+            if plan[2 * s + half]:
+                @pl.when(step == s)
+                def _():
+                    for event in plan[2 * s + half]:
+                        job.forward(event)
+    sends = Sends(sems)
+    branch_sends = [sends.add(gate, gate_o), sends.add(inner, inner_o), sends.add(mixed, mixed_o),
+                    sends.add(ext.at[pl.ds(0, tokens)], normed_o)]
+    gate_sends = [sends.add(rate, rate_o), sends.add(entry, entry_o), sends.add(decay, decay_o), sends.add(pseg, pseg_o)]
+    state_sends = [sends.add(states, states_o), sends.add(sstart, sstart_o), sends.add(swap.land, all_o),
+                   sends.add(gated, gated_o)]
+    last_sends = [sends.add(first, first_o), sends.add(normed2, normed2_o)]
+
+    def start(copies):
+        for copy in copies:
+            copy.start()
+
+    @pl.when(step == 0)
+    def _():
+        greet(job.links, swap)
+        for event in job.events[: len(FFN_GATHER)]:
+            job.forward(event)
+        gain = gain_ref[:1]
+
+        def norm(i, _):
+            at = rows_at(i * CHUNK)
+            value = x_ref[at].astype(F32)
+            ext[at] = (value * inverse_norm(value, depth) * gain).astype(BF16)
+            return 0
+        lax.fori_loop(0, tokens // CHUNK, norm, 0)
+        rim = rim_ref[...].astype(F32)
+        ext[pl.ds(tokens, rim.shape[0])] = (rim * inverse_norm(rim, depth) * gain).astype(BF16)
+
+    @pl.when(step < parts)
+    def _():
+        j = jnp.minimum(step, parts - 1)
+        here = pl.ds(pl.multiple_of(j * W, W), W)
+        pump(0, 0, parts)
+        got = dot(ext[:tokens], wg_ref[...].reshape(depth, W))
+        for t in range(tiles):
+            gate[j * tiles + t] = got[:, lanes(t)]
+        got = dot(ext[...], wi_ref[...].reshape(depth, W))
+        for b in range(batch):
+            inner[b * span : b * span + 8, here] = got[tokens + 8 * b : tokens + 8 * b + 8]
+            inner[b * span + 8 : (b + 1) * span, here] = got[b * width : (b + 1) * width]
+        pump(1, 0, parts)
+        for b in range(batch):
+            conv = vec_ref[CONV_BIAS : CONV_BIAS + 1, here]
+            for lag in range(4):
+                conv = conv + vec_ref[lag : lag + 1, here] * inner[b * span + 8 - lag : (b + 1) * span - lag, here]
+            mixed[b * width : (b + 1) * width, here] = conv.astype(BF16)
+
+    @pl.when(step == parts - 1)
+    def _():
+        start(branch_sends)
+
+    @pl.when(jnp.logical_and(step >= parts, step < 2 * parts))
+    def _():
+        j = jnp.clip(step - parts, 0, parts - 1)
+        pump(0, parts, 2 * parts)
+        for w_ref, to in ((wr_ref, rate), (we_ref, entry)):
+            got = dot(mixed[...], w_ref[...].reshape(r, W))
+            for t in range(tiles):
+                to[j * tiles + t] = got[:, lanes(t)]
+        pump(1, parts, 2 * parts)
+
+        def gating(t, b, spot, at, cols, _):
+            g = j * tiles + t
+            tile = pl.ds(pl.multiple_of(j * W + t * LANES, LANES), LANES)
+            a_rate = sigmoid(rate[g, at] + vec_ref[RATE_BIAS : RATE_BIAS + 1, tile])
+            an_entry = sigmoid(entry[g, at] + vec_ref[ENTRY_BIAS : ENTRY_BIAS + 1, tile])
+            log_decay = vec_ref[COEF : COEF + 1, tile] * a_rate
+            z = 2.0 * log_decay
+            root = jnp.sqrt(one_less_exp(z, jnp.exp(z)))
+            valid = in_row(spot, width, a_rate.shape) < info_ref[b]
+            rate[g, at] = a_rate
+            entry[g, at] = an_entry
+            decay[g, at] = jnp.where(valid, jnp.exp(log_decay), 1.0)
+            drive[g, at] = jnp.where(valid, root * an_entry * mixed[at, tile].astype(F32), 0.0)
+            return 0
+        each_tile(batch, width, tiles, gating)
+        for t in range(tiles):
+            g = j * tiles + t
+            tile = pl.ds(pl.multiple_of(j * W + t * LANES, LANES), LANES)
+            for b in range(batch):
+                prod = jnp.ones((SEGS, LANES), F32)
+                state = jnp.zeros((SEGS, LANES), F32)
+                for s in range(width // SEGS):
+                    at = strided(b, width, s)
+                    a = decay[g, at]
+                    state = a * state + drive[g, at]
+                    prod = prod * a
+                pseg[b * SEGS : (b + 1) * SEGS, tile] = prod
+                hseg[b * SEGS : (b + 1) * SEGS, tile] = state
+                whole, end = prod[:1], state[:1]
+                for i in range(1, SEGS):
+                    whole = whole * prod[i : i + 1]
+                    end = prod[i : i + 1] * end + state[i : i + 1]
+                swap.rows[g, b : b + 1] = whole
+                swap.rows[g, batch + b : batch + b + 1] = end
+
+    @pl.when(step == 2 * parts - 1)
+    def _():
+        start(gate_sends)
+        swap.begin()
+
+    @pl.when(step == 2 * parts)
+    def _():
+        swap.finish()
+
+    @pl.when(jnp.logical_and(step >= 2 * parts, step < 3 * parts))
+    def _():
+        j = jnp.clip(step - 2 * parts, 0, parts - 1)
+        me = lax.axis_index("seq")
+        pump(0, 2 * parts, 3 * parts)
+        for t in range(tiles):
+            g = j * tiles + t
+            tile = pl.ds(pl.multiple_of(j * W + t * LANES, LANES), LANES)
+            for b in range(batch):
+                begin = jnp.zeros((1, LANES), F32)
+                for k in range(n_seq):
+                    new = swap.land[k, g, b : b + 1] * begin + swap.land[k, g, batch + b : batch + b + 1]
+                    begin = jnp.where(k < me, new, begin)
+                for i in range(SEGS):
+                    at = b * SEGS + i
+                    sstart[at : at + 1, tile] = begin
+                    begin = pseg[at : at + 1, tile] * begin + hseg[at : at + 1, tile]
+                state = sstart[b * SEGS : (b + 1) * SEGS, tile]
+                for s in range(width // SEGS):
+                    at = strided(b, width, s)
+                    state = decay[g, at] * state + drive[g, at]
+                    states[g, at] = state
+        pump(1, 2 * parts, 3 * parts)
+
+        def gating(t, b, spot, at, cols, _):
+            g = j * tiles + t
+            tile = pl.ds(pl.multiple_of(j * W + t * LANES, LANES), LANES)
+            gated[at, tile] = (states[g, at] * gelu_both(gate[g, at])[0]).astype(BF16)
+            return 0
+        each_tile(batch, width, tiles, gating)
+
+    @pl.when(step == 3 * parts - 1)
+    def _():
+        start(state_sends)
+
+    @pl.when(step >= 3 * parts)
+    def _():
+        half = jnp.clip(step - 3 * parts, 0, halves - 1)
+        here = pl.ds(pl.multiple_of(half * W, W), W)
+        pump(0, 3 * parts, steps)
+        first[:, here] = x_ref[:, here].astype(F32) + dot(gated[...], wo_ref[...].reshape(r, W))
+        pump(1, 3 * parts, steps)
+
+    @pl.when(step == steps - 1)
+    def _():
+        def norm(i, _):
+            at = rows_at(i * CHUNK)
+            value = first[at]
+            normed2[at] = (value * inverse_norm(value, depth) * gain2_ref[:1]).astype(BF16)
+            return 0
+        lax.fori_loop(0, tokens // CHUNK, norm, 0)
+        start(last_sends)
+        job.finish()
+        sends.finish()
+
+
+def forward(info, tokens2, rim, gain, gain2, vec, packed, shard, batch, n_seq):
+    tokens, depth = tokens2.shape
+    width = tokens // batch
+    n = packed.shape[0]
+    r = vec.shape[1]
+    parts, halves, tiles = r // W, depth // W, r // LANES
+    rows, rrows = depth // n, r // n
+    full = lambda a: pl.BlockSpec(a.shape, lambda j: (0,) * a.ndim)
+    anywhere = pl.BlockSpec(memory_space=pl.ANY)
+    clamp = lambda j, low, count: jnp.clip(j - low, 0, count - 1)
+
+    def block(count, at, low, number):
+        return pl.BlockSpec((n, count, W), lambda j: (0, at // count + clamp(j, low, number), 0))
+    S = jax.ShapeDtypeStruct
+    flat, tall, segs = S((tokens, r), BF16), S((tiles, tokens, LANES), F32), S((batch * SEGS, r), F32)
+    inner, ends = S((tokens + 8 * batch, r), F32), S((n_seq, tiles, 2 * batch, LANES), F32)
+    first, normed = S((tokens, depth), F32), S((tokens, depth), BF16)
+    outs = [tall, inner, flat, normed, tall, tall, tall, tall, segs, segs, ends, flat, first, normed,
+            S((n, shard.shape[0], W), BF16)]
+    vm = lambda s: pltpu.VMEM(s.shape, s.dtype)
+    scratch = [pltpu.VMEM((tokens + 8 * batch, depth), BF16)] + [
+        vm(s) for s in (tall, inner, flat, tall, tall, tall, tall, tall, segs, segs, segs, flat, first, normed)]
+    return pl.pallas_call(
+        functools.partial(forward_kernel, batch, width, n_seq),
+        grid=(3 * parts + halves,),
+        in_specs=[pl.BlockSpec(memory_space=pltpu.SMEM), full(tokens2), full(rim), full(gain), full(gain2), full(vec),
+                  block(rows, GATE_AT, 0, parts), block(rows, INPUT_AT, 0, parts),
+                  block(rrows, RATE_AT, parts, parts), block(rrows, ENTRY_AT, parts, parts),
+                  block(rrows, OUT_AT, 3 * parts, halves), anywhere],
+        out_specs=[anywhere] * len(outs),
+        out_shape=outs,
+        scratch_shapes=scratch + [SEM((FORWARD_OUTS + 1,))] + Exchange.scratch(n_seq, (tiles, 2 * batch, LANES))
+        + Gather.scratch(FFN_GATHER),
+        compiler_params=pltpu.CompilerParams(collective_id=3, has_side_effects=True, vmem_limit_bytes=62 << 20),
+    )(info, tokens2, rim, gain, gain2, vec, packed, packed, packed, packed, packed, shard)
+
+
 RATE_AT, ENTRY_AT, OUT_AT, GATE_AT, INPUT_AT, REC_ROWS = 0, 144, 288, 384, 480, 576
-FFN_GATE_AT, FFN_UP_AT, FFN_DOWN_AT, SMALL_AT, SMALL_ROWS = 576, 768, 960, 1152, 16
-GATHER_PARTS = ((0, 0, 0, 288, 0), (0, 0, 288, 288, 1), (0, 0, 576, 288, 2), (0, 0, 864, 304, 3))
+FFN_GATE_AT, FFN_UP_AT, FFN_DOWN_AT, FFN_ROWS, SMALL_ROWS = 0, 192, 384, 576, 16
+REC_GATHER = ((0, 0, 0, 144, 0), (0, 0, 144, 144, 1), (0, 0, 288, 144, 2), (0, 0, 432, 160, 3))
+FFN_GATHER = ((0, 0, 0, 144, 0), (0, 0, 144, 144, 1), (0, 0, 288, 144, 2), (0, 0, 432, 144, 3))
 SCATTER_PARTS = ((0, 0, 288, 0), (0, 288, 288, 1), (1, 0, 288, 2), (1, 288, 288, 3), (2, 0, 16, 0))
 
 
@@ -1583,9 +1649,11 @@
     rim = pad_rows(from_behind(tokens[:, width - 3 :], "seq", 1), 5, 8)
     flat = jnp.concatenate([item.reshape(-1) for item in small])
     flat = jnp.pad(flat, (0, SMALL_ROWS * W - flat.shape[0])).reshape(SMALL_ROWS, W)
-    order = (rate_proj, entry_proj, out_proj, gate_proj, input_proj, ffn_gate, ffn_up, ffn_down)
-    packed = gather(GATHER_PARTS, [jnp.concatenate([pack_blocks(item) for item in order] + [flat], axis=0)], [SMALL_AT + SMALL_ROWS])[0]
-    flats = packed[:, SMALL_AT].astype(jnp.float32)
+    order = (rate_proj, entry_proj, out_proj, gate_proj, input_proj)
+    shard = jnp.concatenate([pack_blocks(item) for item in order] + [flat], axis=0)
+    packed = gather(REC_GATHER, [shard], [REC_ROWS + SMALL_ROWS])[0]
+    shard = jnp.concatenate([pack_blocks(item) for item in (ffn_gate, ffn_up, ffn_down)], axis=0)
+    flats = packed[:, REC_ROWS].astype(jnp.float32)
     lo, vectors = 0, []
     for item in small:
         part = flats[:, lo : lo + item.size]
@@ -1604,14 +1672,10 @@
     tokens2 = tokens.reshape(batch * width, depth)
     cot2 = cotangent.reshape(batch * width, depth)
 
-    gate_pre, inner, mixed, normed = branch(tokens2, rim, norm_gain, packed, vec, batch)
-    rate, entry, decay, drive, pseg, hseg, ends = gates(info, mixed, packed, vec, batch)
-    pall = exchange(ends, n_seq, 3)
-    states, sstart, gated, first, normed_two = states_and_first(
-        info, decay, drive, gate_pre, pseg, hseg, pall, tokens2, packed, ffn_gain, batch)
-    block_out, d_first, d_low, g_ffn_gain, grad_ffn = feed_forward(info, first, normed_two, cot2, ffn_gain, packed, f, batch)
-    d_states, d_gate, gseg, gtot, grad_rec = unproject(d_low, packed, gated, gate_pre, states, decay, pseg, batch)
-    gall = exchange(gtot, n_seq, 4)
+    (gate_pre, inner, mixed, normed, rate, entry, decay, states, pseg, sstart, pall, gated, first, normed_two,
+     packed_ffn) = forward(info, tokens2, rim, norm_gain, ffn_gain, vec, packed, shard, batch, n_seq)
+    block_out, d_first, d_low, g_ffn_gain, grad_ffn = feed_forward(info, first, normed_two, cot2, ffn_gain, packed_ffn, f, batch)
+    d_states, d_gate, gseg, gall, grad_rec = unproject(d_low, packed, gated, gate_pre, states, decay, pseg, batch, n_seq)
     d_mixed, sums, grad_rec = recur_back(
         info, mixed, decay, d_states, states, rate, entry, pseg, gseg, sstart, pall, gall, vec, packed, grad_rec, batch)
     rim_back = from_behind(d_mixed.reshape(batch, width, r)[:, :3].astype(jnp.bfloat16), "seq", -1)
@@ -1631,7 +1695,7 @@
     result = [(at["gate"], gate_proj), (at["input"], input_proj), (at["rate"], rate_proj), (at["entry"], entry_proj),
               (at["out"], out_proj), (0, ffn_gate), (FFN_UP_AT - FFN_GATE_AT, ffn_up), (FFN_DOWN_AT - FFN_GATE_AT, ffn_down)]
     result = [unpack_blocks(total[lo : lo + item.size // W], *item.shape) for lo, item in result]
-    flat = total[SMALL_AT]
+    flat = total[FFN_ROWS + REC_ROWS]
     lo = 0
     for item in small:
         result.append(flat[lo : lo + item.size].reshape(item.shape))

time: 561 us -> 527 us (0.939)
  Pallas kernels: 507 us -> 475 us
    pallas_call x1, Pallas kernels: 146 us -> 79.4 us  [gather(): pl.pallas_call(kernel, out_shape=[jax.ShapeDtypeStruct((8 * ZN, count, W)...]
    pallas_call x5 -> x1, Pallas kernels: 65.9 us -> 90 us  [forward(): pl.pallas_call(functools.partial(forward_kernel, batch, width, n_seq), gr...]
    pallas_call x1, Pallas kernels: 165 us -> 170 us  [scatter(): pl.pallas_call(kernel, out_shape=jax.ShapeDtypeStruct((total, W), jnp.flo...]
  transfers between devices with their start and end apart: 2 -> 2, of which waited for: 1 -> 1; matrix products, arithmetic and copies ran while one was open for 2% -> 3% of each run, Pallas kernels for 26% -> 15%
where the time goes in v2:
time: 527 us; the launch traced here: 521 us
  Pallas kernels  475 us (90%)
  local copies, waits for them, and re-layouts  32.7 us (6%)
  other arithmetic  7.69 us (1%)
    pallas_call x1, Pallas kernels, scatter(): pl.pallas_call(kernel, out_shape=jax.ShapeDtypeStruct((total, W), jnp.flo...  170 us
    pallas_call x1, Pallas kernels, forward(): pl.pallas_call(functools.partial(forward_kernel, batch, width, n_seq), gr...  90 us
    pallas_call x1, Pallas kernels, gather(): pl.pallas_call(kernel, out_shape=[jax.ShapeDtypeStruct((8 * ZN, count, W)...  79.4 us
    pallas_call x1, Pallas kernels, feed_forward(): pl.pallas_call(functools.partial(ffn_kernel, batch, width), grid=(nd + nw...  58.9 us
    pallas_call x1, Pallas kernels, recur_back(): pl.pallas_call(functools.partial(recur_kernel, batch, width, n_seq), grid...  33.3 us
    pallas_call x1, Pallas kernels, unproject(): pl.pallas_call(functools.partial(unproject_kernel, batch, width), grid=(n...  22.1 us
    pallas_call x1, Pallas kernels, entry_back(): pl.pallas_call(functools.partial(entry_kernel, batch, width), grid=(r //...  21.1 us
  transfers between devices with their start and end apart: 2, of which 1 were waited for; matrix products, arithmetic and copies ran while one was open for 3% of the time, Pallas kernels for 15%

profile of v2, /device:TPU:16, one launch (start us, length us, event | category | flops | bytes accessed | tf_op | source)
XLA Modules:
  0.0 521.4 jit_solution(1120591886188057991)
XLA Ops:
  1.4 1.7 collective-permute-start
  3.9 4.1 concatenate.20
  8.1 0.9 copy.92
  9.0 1.0 reshape.294
  10.0 1.0 reshape.296
  11.0 1.0 reshape.288
  12.0 1.0 reshape.290
  13.2 0.8 copy-done
  14.0 79.4 %shard_map.305.wg_ref.wi_ref.wr_ref.we_ref.wo_ref = bf16[32,592,512]{2,1,0:T(8,128)(2,1)} custom-call(bf16[592,512]{1,0:T(8,128)(2,1)} %copy-done), custom_call_target="tpu_custom_call" | custom-call | tf_op jit(solution)/shard_map/pallas_call | solution.py:1216
  93.5 1.0 slice_convert_fusion
  95.5 0.9 pad_maximum_fusion.shard_ref
  97.8 1.3 concatenate.22.vec_ref
  100.9 90.0 %shard_map.306 = (f32[12,512,128]{2,1,0:T(8,128)}, f32[528,1536]{1,0:T(8,128)}, bf16[512,1536]{1,0:T(8,128)(2,1)}, bf16[512,1024]{1,0:T(8,128)(2,1)}, f32[12,512...) custom-call(s32[3]{0:T(128)} %pad_add_fusion.info_ref, ...), custom_call_target="tpu_custom_call" | custom-call | tf_op jit(solution)/shard_map/pallas_call | solution.py:1605
  190.9 58.9 %shard_map.307 = (f32[512,1024]{1,0:T(8,128)}, f32[512,1024]{1,0:T(8,128)}, bf16[512,1024]{1,0:T(8,128)(2,1)}, f32[8,1024]{1,0:T(8,128)}, bf16[32,576,512]{2,1,0:T(8,128)(2,1)}) custom-call(s32[3]{0:T(128)} %pad_add_fusion.info_ref, f32[512,1024]{1,0:T(8,128)} %get-tuple-element.49.first_ref, bf16[512,1024]{1,0:T(8,128)(2,1)} %get-tuple-element.50.normed_ref, ...), custom_call_target="tpu_custom_call" | custom-call | tf_op jit(solution)/shard_map/pallas_call | solution.py:723
  249.8 22.1 %shard_map.308 = (f32[12,512,128]{2,1,0:T(8,128)}, bf16[512,1536]{1,0:T(8,128)(2,1)}, f32[16,1536]{1,0:T(8,128)}, f32[8,12,2,128]{3,2,1,0:T(2,128)}, bf16[32,576,512]{2,1,0:T(8,128)(2,1)}) custom-call(bf16[512,1024]{1,0:T(8,128)(2,1)} %get-tuple-element.55.dlow_ref, bf16[32,592,512]{2,1,0:T(8,128)(2,1)} %shard_map.305.wg_ref.wi_ref.wr_ref.we_ref.wo_ref, ...), custom_call_target="tpu_custom_call" | custom-call | tf_op jit(solution)/shard_map/pallas_call | solution.py:798
  271.9 33.3 %shard_map.309 = (f32[512,1536]{1,0:T(8,128)}, f32[8,1536]{1,0:T(8,128)}, bf16[32,576,512]{2,1,0:T(8,128)(2,1)}) custom-call(s32[3]{0:T(128)} %pad_add_fusion.info_ref, bf16[512,1536]{1,0:T(8,128)(2,1)} %get-tuple-element.53.mixed_ref, f32[12,512,128]{2,1,0:T(8,128)} %get-tuple-element.54.decay_ref, ...), custom_call_target="tpu_custom_call", output_to_operand_aliasing={{2}: (15, {})} | custom-call | tf_op jit(solution)/shard_map/pallas_call | solution.py:914
  305.3 0.8 convert.41
  306.1 2.1 convert.37
  308.2 1.3 collective-permute-start.1
  309.9 1.4 collective-permute-done.1
  311.9 21.1 %shard_map.310 = (f32[8,1536]{1,0:T(8,128)}, f32[512,1024]{1,0:T(8,128)}, f32[8,1024]{1,0:T(8,128)}, bf16[32,576,512]{2,1,0:T(8,128)(2,1)}) custom-call(f32[512,1536]{1,0:T(8,128)} %get-tuple-element.68.dmixed_ref, f32[16,1536]{1,0:T(8,128)} %bitcast_convert_fusion.rim_ref, ...), custom_call_target="tpu_custom_call", output_to_operand_aliasing={{3}: (11, {})} | custom-call | tf_op jit(solution)/shard_map/pallas_call | solution.py:994
  333.1 0.8 convert.40
  335.2 1.0 copy.78
  336.2 170.4 %shard_map.311 = f32[1168,512]{1,0:T(8,128)} custom-call(bf16[32,576,512]{2,1,0:T(8,128)(2,1)} %get-tuple-element.75.refs_0_, bf16[32,576,512]{2,1,0:T(8,128)(2,1)} %get-tuple-element.76.refs_1_, bf16[32,16,512]{2,1,0:T(8,128)(2,1)} %bitcast.98), custom_call_target="tpu_custom_call" | custom-call | tf_op jit(solution)/shard_map/pallas_call | solution.py:1365
  506.6 0.8 slice_reduce_fusion.4
  507.4 1.3 slice_bitcast_fusion.4
  508.8 1.4 slice_bitcast_fusion
  510.1 1.2 fusion.2
  511.3 1.1 fusion.3
  512.4 1.3 fusion.1
  518.6 0.8 copy.81
  519.6 0.8 copy.82
  (81 shorter events, 14.2 us)
Async XLA Ops:
  1.4 97.7 %collective-permute-start = (bf16[2,3,1024]{2,1,0:T(4,128)(2,1)S(1)}, bf16[2,3,1024]{2,1,0:T(4,128)(2,1)S(1)}, u32[]{:S(2)}, u32[]{:S(2)}) collective-permute-start(bf16[2,3,1024]{2,1,0:T(4,128)(2,1)S(1)} %slice.123), channel_id=1, source_target_pairs={{0,4},{4,8},{8,12},{12,16},{16,20},{20,24},{24,28},{1,5},{5,9},{9,... | collective-permute-start | bytes 36872 | tf_op jit(solution)/shard_map/ppermute | solution.py:20
  13.2 0.8 copy-start
  14.0 80.7 %copy-start.3 = (bf16[96,1024]{1,0:T(8,128)(2,1)S(1)}, bf16[96,1024]{1,0:T(8,128)(2,1)}, u32[]{:S(2)}) copy-start(bf16[96,1024]{1,0:T(8,128)(2,1)} %param.28) | copy-start | bytes 589828
  14.0 80.7 %copy-start.1 = (bf16[32,3072]{1,0:T(8,128)(2,1)S(1)}, bf16[32,3072]{1,0:T(8,128)(2,1)}, u32[]{:S(2)}) copy-start(bf16[32,3072]{1,0:T(8,128)(2,1)} %param.26) | copy-start | bytes 589828
  14.0 81.0 %copy-start.2 = (bf16[32,3072]{1,0:T(8,128)(2,1)S(1)}, bf16[32,3072]{1,0:T(8,128)(2,1)}, u32[]{:S(2)}) copy-start(bf16[32,3072]{1,0:T(8,128)(2,1)} %param.27) | copy-start | bytes 589828
  93.5 2.0 copy-start.5
  306.1 3.5 copy-start.4
  308.2 3.1 collective-permute-start.1
